TPU v7x, 512 devices: a whole 4x8x8 slice. The times are simulated.
512 devices in a mesh: ctx: 64 (over z, y), head: 8 (over x, core).
Axes of the slice: x: 4, y: 8, z: 8, core: 2. Of those that a mesh axis runs over, the one named last changes fastest.
Arguments:
- queries: bfloat16 [2, 64, 16384], P(None, 'ctx', 'head'), may hold values from -6 to 6
- prompt_keys: bfloat16 [32768, 1024], P('ctx', 'head'), may hold values from -6 to 6
- prompt_values: bfloat16 [32768, 1024], P('ctx', 'head'), may hold values from -6 to 6
- selected: int32 [64, 8, 512], P(None, 'head', 'ctx'), may hold values from -1 to 7, as said below
- cache_keys: bfloat16 [64, 256, 1024], P('ctx', None, 'head'), may hold values from -6 to 6
- cache_values: bfloat16 [64, 256, 1024], P('ctx', None, 'head'), may hold values from -6 to 6
- new_keys: bfloat16 [2, 64, 1024], P(None, 'ctx', 'head'), may hold values from -6 to 6
- new_values: bfloat16 [2, 64, 1024], P(None, 'ctx', 'head'), may hold values from -6 to 6
- positions: int32 [64], P('ctx'), may hold values from 1 to 256, as said below
- out_weight: bfloat16 [16384, 16384], P('head', 'ctx'), may hold values from -0.375 to 0.375
Outputs:
- mixed: bfloat16 [2, 64, 16384], P(None, 'head', 'ctx')
Inputs may be any that keep to these rules, and one draw needn't show every extreme that they name: `selected`: entry [r, g, k * 8 + i] is the i-th block that sample r selects for key-value head g on context shard k, numbered within the shard; a sample's blocks on one shard are distinct, and -1 marks unused slots, which follow the used ones. Some sample fills all 8 slots of some shard. `positions`: some sample has 256 cached tokens.
All inputs are finite; a program needn't handle non-finite values.
Results may differ from a plain program's by a relative error of at most 0.005.
Values may be sent and summed in bfloat16 or wider, within the bound.
No kernel may reach another device: no remote copies, remote signals or barrier semaphores. Data moves between devices by JAX's collectives and lax.ppermute only.
A program may use at most 64 MiB of HBM per device.

v0:
```python
import math

import jax
import jax.numpy as jnp
from jax import lax
from jax.sharding import PartitionSpec as P

H = 128
KVH = 8
HD = 128
BLOCK = 64


NEGATIVE = -1e30


def own_partial(query_rows, cache_keys, cache_values, new_keys, new_values, positions):
    step_count, row_count, group_count, per_group, head_dim = query_rows.shape
    score_scale = 1.0 / math.sqrt(head_dim)
    slot_total = cache_keys.shape[1]
    new_total = new_keys.shape[0]
    cache_key_rows = cache_keys.reshape(row_count, slot_total, group_count, head_dim)
    cache_value_rows = cache_values.reshape(row_count, slot_total, group_count, head_dim)
    new_key_rows = new_keys.reshape(new_total, row_count, group_count, head_dim)
    new_value_rows = new_values.reshape(new_total, row_count, group_count, head_dim)
    cache_scores = (
        jnp.einsum(
            "srgqd,rjgd->srgqj", query_rows, cache_key_rows, preferred_element_type=jnp.float32
        )
        * score_scale
    )
    new_scores = (
        jnp.einsum(
            "srgqd,trgd->srgqt", query_rows, new_key_rows, preferred_element_type=jnp.float32
        )
        * score_scale
    )
    cache_alive = (jnp.arange(slot_total, dtype=jnp.int32)[None, :] < positions[:, None])[
        None, :, None, None, :
    ]
    new_alive = (
        jnp.arange(new_total, dtype=jnp.int32)[None, :]
        <= jnp.arange(step_count, dtype=jnp.int32)[:, None]
    )[:, None, None, None, :]
    top_score = jnp.maximum(
        jnp.max(jnp.where(cache_alive, cache_scores, NEGATIVE), axis=-1),
        jnp.max(jnp.where(new_alive, new_scores, NEGATIVE), axis=-1),
    )
    cache_weights = jnp.where(cache_alive, jnp.exp(cache_scores - top_score[..., None]), 0.0)
    new_weights = jnp.where(new_alive, jnp.exp(new_scores - top_score[..., None]), 0.0)
    mass_sum = jnp.sum(cache_weights, axis=-1) + jnp.sum(new_weights, axis=-1)
    output = jnp.einsum(
        "srgqj,rjgd->srgqd",
        cache_weights.astype(jnp.bfloat16),
        cache_value_rows,
        preferred_element_type=jnp.float32,
    )
    output = output + jnp.einsum(
        "srgqt,trgd->srgqd",
        new_weights.astype(jnp.bfloat16),
        new_value_rows,
        preferred_element_type=jnp.float32,
    )
    return (output, top_score, mass_sum)


def prompt_partial(gathered, prompt_keys, prompt_values, block_mask):
    step_count, row_count = (gathered.shape[0], gathered.shape[1])
    token_count = prompt_keys.shape[0]
    group_count = prompt_keys.shape[1] // HD
    per_group = H // KVH
    block_count = token_count // BLOCK
    score_scale = 1.0 / math.sqrt(HD)
    key_rows = prompt_keys.reshape(token_count, group_count, HD)
    value_rows = prompt_values.reshape(token_count, group_count, HD)
    block_rows = math.gcd(row_count, max(1, 512 // (step_count * per_group)))
    block_total = row_count // block_rows
    query_blocks = jnp.moveaxis(
        gathered.reshape(step_count, block_total, block_rows, group_count, per_group, HD), 1, 0
    )
    mask_blocks = block_mask.reshape(block_total, block_rows, group_count, block_count)

    def one_block(block_args):
        query_part, mask_part = block_args
        scores = (
            jnp.einsum("srgqd,tgd->srgqt", query_part, key_rows, preferred_element_type=jnp.float32)
            * score_scale
        )
        scores = scores.reshape(step_count, block_rows, group_count, per_group, block_count, BLOCK)
        alive_mask = mask_part[None, :, :, None, :, None]
        top_score = jnp.max(jnp.where(alive_mask, scores, NEGATIVE), axis=(-2, -1))
        weights = jnp.where(alive_mask, jnp.exp(scores - top_score[..., None, None]), 0.0)
        mass_sum = jnp.sum(weights, axis=(-2, -1))
        flat_weights = weights.astype(jnp.bfloat16).reshape(
            step_count, block_rows, group_count, per_group, token_count
        )
        output = jnp.einsum(
            "srgqt,tgd->srgqd", flat_weights, value_rows, preferred_element_type=jnp.float32
        )
        return (output, top_score, mass_sum)

    output, top_score, mass_sum = lax.map(one_block, (query_blocks, mask_blocks))
    output = jnp.moveaxis(output, 0, 1).reshape(step_count, row_count, group_count * per_group * HD)
    top_score = jnp.moveaxis(top_score, 0, 1).reshape(
        step_count, row_count, group_count * per_group
    )
    mass_sum = jnp.moveaxis(mass_sum, 0, 1).reshape(step_count, row_count, group_count * per_group)
    return (output, top_score, mass_sum)


def shards(
    queries,
    prompt_keys,
    prompt_values,
    selected,
    cache_keys,
    cache_values,
    new_keys,
    new_values,
    positions,
    out_weight,
):
    step_count = queries.shape[0]
    rows_here = queries.shape[1]
    group_count = prompt_keys.shape[1] // HD
    per_group = H // KVH
    heads_here = group_count * per_group
    block_count = prompt_keys.shape[0] // BLOCK
    block_mask = jnp.any(
        selected[..., None] == jnp.arange(block_count, dtype=jnp.int32)[None, None, None, :], axis=2
    )
    own_queries = queries.reshape(step_count, rows_here, group_count, per_group, HD)
    own_out, own_top, own_mass = own_partial(
        own_queries, cache_keys, cache_values, new_keys, new_values, positions
    )
    pieces = []
    for step_index in range(step_count):
        gathered = lax.all_gather(queries[step_index : step_index + 1], "ctx", axis=1, tiled=True)
        pieces.append(prompt_partial(gathered, prompt_keys, prompt_values, block_mask))
    part_out = jnp.concatenate([entry[0] for entry in pieces], axis=0)
    part_top = jnp.concatenate([entry[1] for entry in pieces], axis=0)
    part_mass = jnp.concatenate([entry[2] for entry in pieces], axis=0)
    shard_count = lax.axis_size("ctx")
    out_sent = part_out.reshape(1, step_count, shard_count, rows_here, heads_here * HD)
    top_sent = part_top.reshape(1, step_count, shard_count, rows_here, heads_here)
    mass_sent = part_mass.reshape(1, step_count, shard_count, rows_here, heads_here)
    shard_out = lax.all_to_all(out_sent, "ctx", split_axis=2, concat_axis=0, tiled=True)
    shard_tops = lax.all_to_all(top_sent, "ctx", split_axis=2, concat_axis=0, tiled=True)
    shard_masses = lax.all_to_all(mass_sent, "ctx", split_axis=2, concat_axis=0, tiled=True)
    item_count = shard_out.shape[3]
    tops_here = shard_tops[:, :, 0]
    masses_here = shard_masses[:, :, 0]
    shard_top = jnp.max(tops_here, axis=0)
    factor = jnp.exp(tops_here - shard_top[None])
    shard_mass = jnp.sum(factor * masses_here, axis=0)
    widened = shard_out[:, :, 0].reshape(shard_out.shape[0], step_count, item_count, heads_here, HD)
    shard_sum = jnp.sum(factor[..., None] * widened, axis=0).reshape(
        step_count, item_count, heads_here * HD
    )
    shard_sum, shard_top, shard_mass = (shard_sum, shard_top, shard_mass)
    group_top = own_top.reshape(step_count, rows_here, heads_here)
    group_mass = own_mass.reshape(step_count, rows_here, heads_here)
    best_score = jnp.maximum(shard_top, group_top)
    shard_factor = jnp.exp(shard_top - best_score)
    own_factor = jnp.exp(group_top - best_score)
    numer = shard_sum.reshape(step_count, rows_here, heads_here, HD) * shard_factor[..., None]
    numer = numer + own_out.reshape(step_count, rows_here, heads_here, HD) * own_factor[..., None]
    denom = shard_mass * shard_factor + group_mass * own_factor
    attended = (
        (numer / denom[..., None])
        .astype(jnp.bfloat16)
        .reshape(step_count, rows_here, heads_here * HD)
    )
    piece = lax.all_gather(attended, "ctx", axis=1, tiled=True)
    item_count = piece.shape[1]
    flattened = piece.reshape(step_count * item_count, piece.shape[2])
    product = jnp.dot(flattened, out_weight, preferred_element_type=jnp.float32)
    terms = product.reshape(step_count, item_count, out_weight.shape[1])
    mixed = lax.psum_scatter(terms, "head", scatter_dimension=1, tiled=True)
    return mixed.astype(jnp.bfloat16)


def solution(mesh):
    placed = (
        P(None, "ctx", "head"),
        P("ctx", "head"),
        P("ctx", "head"),
        P(None, "head", "ctx"),
        P("ctx", None, "head"),
        P("ctx", None, "head"),
        P(None, "ctx", "head"),
        P(None, "ctx", "head"),
        P("ctx"),
        P("head", "ctx"),
    )
    return jax.shard_map(
        shards, mesh=mesh, in_specs=placed, out_specs=P(None, "head", "ctx"), check_vma=False
    )
```

profile of v0, /device:TPU:1, one launch (start us, length us, event | category | flops | bytes accessed | tf_op | source)
XLA Modules:
  0.0 273.2 jit_solution(6289194565924472848)
XLA Ops:
  6.5 0.8 copy-done.5
  7.3 0.1 copy.81
  7.5 45.7 %all_gather.9 = bf16[1,64,2048]{2,0,1:T(2,128)(2,1)S(1)} all-gather(bf16[1,1,2048]{2,0,1:T(2,128)(2,1)S(1)} %get-tuple-element.238), channel_id=1, replica_groups=mesh['ctx'=64,'head'=8] {'ctx'}, dimensions={1}, use_global_device_ids=true | all-gather | bytes 266240 | tf_op jit(solution)/shard_map/all_gather | solution.py:138
  53.2 1.5 reduce.19
  54.7 36.0 %all_gather.10 = bf16[1,64,2048]{2,0,1:T(2,128)(2,1)S(1)} all-gather(bf16[1,1,2048]{2,0,1:T(2,128)(2,1)S(1)} %get-tuple-element.239), channel_id=1, replica_groups=mesh['ctx'=64,'head'=8] {'ctx'}, dimensions={1}, use_global_device_ids=true | all-gather | bytes 266240 | tf_op jit(solution)/shard_map/all_gather | solution.py:138
  90.8 1.5 reduce.20
  92.4 0.8 copy-done.1
  93.2 0.1 copy-done.8
  93.3 2.8 %while.29 = (s32[]{:T(128)}, f32[2,1,32,1,16,128]{5,4,2,3,1,0:T(8,128)S(1)}, f32[2,1,32,1,16]{4,2,3,1,0:T(8,128)S(1)}, f32[2,1,32,1,16]{4,2,3,1,0:T(8,128)S(1)},...) while((s32[]{:T(128)}, ...), condition=%wide.region_8.9_spmd, body=%wide.region_5.8_spmd.sunk | while | flops 136576000 | bytes 3988341 | solution.py:102
  93.3 0.1 broadcast_in_dim.205
  93.4 0.1 broadcast_in_dim.206
  93.5 0.4 select_reduce_fusion.6
  93.9 0.4 fusion.85
  94.3 0.4 fusion.84
  94.7 0.1 broadcast_in_dim.205
  94.8 0.1 broadcast_in_dim.206
  94.9 0.4 select_reduce_fusion.6
  95.3 0.4 fusion.85
  95.7 0.4 fusion.84
  96.1 0.1 copy.78
  96.2 2.8 %while.28 = (s32[]{:T(128)}, f32[2,1,32,1,16,128]{5,4,2,3,1,0:T(8,128)S(1)}, f32[2,1,32,1,16]{4,2,3,1,0:T(8,128)S(1)}, f32[2,1,32,1,16]{4,2,3,1,0:T(8,128)S(1)},...) while((s32[]{:T(128)}, ...), condition=%wide.region_4.5_spmd, body=%wide.region_1.4_spmd.sunk | while | flops 136576000 | bytes 3988341 | solution.py:102
  96.3 0.1 broadcast_in_dim.197
  96.4 0.1 broadcast_in_dim.198
  96.5 0.4 select_reduce_fusion.5
  96.9 0.4 fusion.81
  97.2 0.4 fusion.80
  97.7 0.1 broadcast_in_dim.197
  97.8 0.1 broadcast_in_dim.198
  97.9 0.4 select_reduce_fusion.5
  98.3 0.4 fusion.81
  98.7 0.4 fusion.80
  99.1 0.1 copy.77
  99.1 0.7 copy.70
  99.8 7.2 %all-to-all-start = ((f32[1,2,64,1,16]{4,1,3,0,2:T(2,128)}), f32[1,2,64,1,16]{4,1,3,0,2:T(2,128)S(1)}, u32[]{:S(2)}, u32[]{:S(2)}) async-start(f32[1,2,64,1,16]{4,1,3,0,2:T(2,128)} %bitcast.43), calls=%async_computation | async-start | bytes 131072 | tf_op jit(solution)/shard_map/all_to_all | solution.py:148
  107.2 0.7 copy.75
  108.0 10.4 %all-to-all-done = f32[1,2,64,1,16]{4,1,3,0,2:T(2,128)S(1)} async-done(((f32[1,2,64,1,16]{4,1,3,0,2:T(2,128)}), f32[1,2,64,1,16]{4,1,3,0,2:T(2,128)S(1)}, u32[]{:S(2)}, u32[]{:S(2)}) %all-to-all-start) | async-done | bytes 8224 | tf_op jit(solution)/shard_map/all_to_all | solution.py:148
  118.4 4.6 %all-to-all-start.2 = ((f32[1,2,64,1,16]{4,1,3,0,2:T(2,128)}), f32[1,2,64,1,16]{4,1,3,0,2:T(2,128)S(1)}, u32[]{:S(2)}, u32[]{:S(2)}) async-start(f32[1,2,64,1,16]{4,1,3,0,2:T(2,128)} %copy.75), calls=%async_computation.2 | async-start | bytes 131072 | tf_op jit(solution)/shard_map/all_to_all | solution.py:149
  123.0 1.9 maximum_bitcast_fusion
  124.9 9.1 %all-to-all-done.2 = f32[1,2,64,1,16]{4,1,3,0,2:T(2,128)S(1)} async-done(((f32[1,2,64,1,16]{4,1,3,0,2:T(2,128)}), f32[1,2,64,1,16]{4,1,3,0,2:T(2,128)S(1)}, u32[]{:S(2)}, u32[]{:S(2)}) %all-to-all-start.2) | async-done | bytes 8224 | tf_op jit(solution)/shard_map/all_to_all | solution.py:149
  134.1 4.7 %all-to-all-start.1 = ((f32[1,2,64,1,2048]{4,1,3,0,2:T(2,128)}), f32[1,2,64,1,2048]{4,1,3,0,2:T(2,128)S(1)}, u32[]{:S(2)}, u32[]{:S(2)}) async-start(f32[1,2,64,1,2048]{4,1,3,0,2:T(2,128)} %maximum_bitcast_fusion), calls=%async_computation.1 | async-start | bytes 2097152 | tf_op jit(solution)/shard_map/all_to_all | solution.py:147
  138.7 0.2 reduce-scatter.2.cloned.1.call-start
  139.6 0.6 copy-done.7
  140.3 0.1 convolution_multiply_fusion.3
  140.4 0.1 fusion.55
  140.5 0.2 select_reduce_fusion.2
  140.8 0.1 fusion.66
  140.9 0.3 copy-done.3
  141.1 0.2 fusion.39
  141.3 0.7 copy-done.6
  142.0 0.2 fusion.31
  142.2 0.2 bitcast_reduce_fusion.1
  142.4 0.1 bitcast_reduce_fusion
  142.4 0.1 fusion.36
  142.5 0.1 div.19
  142.6 0.1 mul.136
  142.7 0.1 mul.139
  142.9 1.4 mul.126
  144.2 1.8 mul.127
  146.0 11.5 %all-to-all-done.1 = f32[1,2,64,1,2048]{4,1,3,0,2:T(2,128)S(1)} async-done(((f32[1,2,64,1,2048]{4,1,3,0,2:T(2,128)}), f32[1,2,64,1,2048]{4,1,3,0,2:T(2,128)S(1)}, u32[]{:S(2)}, u32[]{:S(2)}) %all-to-all-start.1) | async-done | bytes 1048608 | tf_op jit(solution)/shard_map/all_to_all | solution.py:147
  157.5 1.0 fusion.32
  158.5 43.1 %all_gather.11 = bf16[2,64,2048]{2,0,1:T(2,128)(2,1)S(1)} all-gather(bf16[2,1,2048]{2,0,1:T(2,128)(2,1)S(1)} %fusion.50), channel_id=1, replica_groups=mesh['ctx'=64,'head'=8] {'ctx'}, dimensions={1}, use_global_device_ids=true | all-gather | bytes 532480 | tf_op jit(solution)/shard_map/all_gather | solution.py:174
  201.7 1.0 fusion.33
  202.7 62.3 %reduce-scatter.2.cloned.1.call-done = f32[2,8,256]{2,1,0:T(8,128)} async-done(((f32[2,64,256]{2,1,0:T(8,128)}), f32[2,8,256]{2,1,0:T(8,128)}) %reduce-scatter.2.cloned.1.call-update) | async-done | bytes 16400 | tf_op jit(solution)/shard_map/reduce_scatter | solution.py:179
  265.0 1.3 convert_element_type.36
  (45 shorter events, 0.6 us)
Async XLA Ops:
  6.5 195.1 %copy-start = (bf16[2048,256]{1,0:T(8,128)(2,1)S(1)}, bf16[2048,256]{1,0:T(8,128)(2,1)}, u32[]{:S(2)}) copy-start(bf16[2048,256]{1,0:T(8,128)(2,1)} %param.23) | copy-start | bytes 3145732
  6.5 0.8 copy-start.5
  6.5 0.9 copy-start.2
  92.3 0.9 copy-start.1
  92.3 1.0 copy-start.8
  99.8 18.5 %all-to-all-start = ((f32[1,2,64,1,16]{4,1,3,0,2:T(2,128)}), f32[1,2,64,1,16]{4,1,3,0,2:T(2,128)S(1)}, u32[]{:S(2)}, u32[]{:S(2)}) async-start(f32[1,2,64,1,16]{4,1,3,0,2:T(2,128)} %bitcast.43), calls=%async_computation | async-start | bytes 131072 | tf_op jit(solution)/shard_map/all_to_all | solution.py:148
  118.4 15.7 %all-to-all-start.2 = ((f32[1,2,64,1,16]{4,1,3,0,2:T(2,128)}), f32[1,2,64,1,16]{4,1,3,0,2:T(2,128)S(1)}, u32[]{:S(2)}, u32[]{:S(2)}) async-start(f32[1,2,64,1,16]{4,1,3,0,2:T(2,128)} %copy.75), calls=%async_computation.2 | async-start | bytes 131072 | tf_op jit(solution)/shard_map/all_to_all | solution.py:149
  124.9 15.6 %copy-start.4 = (bf16[1,256,128]{2,1,0:T(8,128)(2,1)S(1)}, bf16[1,256,128]{2,1,0:T(8,128)(2,1)}, u32[]{:S(2)}) copy-start(bf16[1,256,128]{2,1,0:T(8,128)(2,1)} %param.18) | copy-start | bytes 196612
  134.1 23.5 %all-to-all-start.1 = ((f32[1,2,64,1,2048]{4,1,3,0,2:T(2,128)}), f32[1,2,64,1,2048]{4,1,3,0,2:T(2,128)S(1)}, u32[]{:S(2)}, u32[]{:S(2)}) async-start(f32[1,2,64,1,2048]{4,1,3,0,2:T(2,128)} %maximum_bitcast_fusion), calls=%async_computation.1 | async-start | bytes 2097152 | tf_op jit(solution)/shard_map/all_to_all | solution.py:147
  138.7 126.3 %reduce-scatter.2.cloned.1.call-start = ((), (), s32[]{:S(2)}) async-start(), calls=%async_computation.4 | async-start | bytes 147456 | tf_op jit(solution)/shard_map/reduce_scatter | solution.py:179
  139.6 0.7 copy-start.7
  140.3 0.8 copy-start.3
  141.3 0.7 copy-start.6
Sparse Core Ops, SparseCore 0:
  202.8 62.1 reduce-scatter.1
where the time goes:
time: 274 us; the launch traced here: 273 us
  blocking collectives  125 us (46%)
  waiting for transfers between devices  93.4 us (34%)
  starting transfers between devices  16.7 us (6%)
  between operations  14.3 us (5%)
  local copies, waits for them, and re-layouts  9.61 us (4%)
  other arithmetic  9.32 us (3%)
  matrix products  4.76 us (2%)
    all_gather x2, blocking collectives, shards(): lax.all_gather(queries[step_index:step_index + 1], 'ctx', axis=1, tiled=T...  81.7 us
    reduce_scatter x1, waiting for transfers between devices, shards(): mixed = lax.psum_scatter(terms, 'head', scatter_dimension=1, tiled=True)  62.3 us
    all_gather x1, blocking collectives, shards(): piece = lax.all_gather(attended, 'ctx', axis=1, tiled=True)  43.1 us
    all_to_all x1, waiting for transfers between devices, shards(): lax.all_to_all(out_sent, 'ctx', split_axis=2, concat_axis=0, tiled=True)  11.5 us
    all_to_all x1, waiting for transfers between devices, shards(): lax.all_to_all(top_sent, 'ctx', split_axis=2, concat_axis=0, tiled=True)  10.4 us
    all_to_all x1, waiting for transfers between devices, shards(): lax.all_to_all(mass_sent, 'ctx', split_axis=2, concat_axis=0, tiled=True)  9.14 us
    all_to_all x1, starting transfers between devices, shards(): lax.all_to_all(top_sent, 'ctx', split_axis=2, concat_axis=0, tiled=True)  7.25 us
  transfers between devices with their start and end apart: 4, of which 4 were waited for; matrix products, arithmetic and copies ran while one was open for 3% of the time, Pallas kernels for 0%

commit v1 on v0

v1 whole, which is shorter than its diff:
```python
import math

import jax
import jax.numpy as jnp
from jax import lax
from jax.experimental import pallas as pl
from jax.experimental.pallas import tpu as pltpu
from jax.sharding import PartitionSpec as P

HD = 128
PER = 16
BLOCK = 64
STEPS = 2
ITEM = STEPS * PER
STAT = 8
NEGATIVE = -1e30
SCALE = math.log2(math.e) / math.sqrt(HD)
TILE = 8

VMEM = pl.BlockSpec(memory_space=pltpu.VMEM)
SMEM = pl.BlockSpec(memory_space=pltpu.SMEM)
PARAMS = pltpu.CompilerParams(vmem_limit_bytes=24 * 1024 * 1024)
F32 = jnp.float32
BF16 = jnp.bfloat16


def dot(a, b):
    return lax.dot_general(a, b, (((1,), (0,)), ((), ())), preferred_element_type=F32)


def dot_t(a, b):
    return lax.dot_general(a, b, (((1,), (1,)), ((), ())), preferred_element_type=F32)


def iota(shape, dim):
    return lax.broadcasted_iota(jnp.int32, shape, dim)


def item_rows(q_ref, rows_ref):
    whole = q_ref[...].astype(F32)
    for step in range(STEPS):
        for head in range(PER):
            row = step * PER + head
            rows_ref[row : row + 1, :] = whole[step : step + 1, head * HD : (head + 1) * HD]
    return rows_ref[...]


def to_lanes(column, count):
    shape = (count, ITEM, HD)
    pick = iota(shape, 1) == iota(shape, 2) % ITEM
    return jnp.sum(jnp.where(pick, column.reshape(shape), 0.0), axis=1)


def spread_kernel(q_ref, out_ref, rows_ref):
    rows = item_rows(q_ref, rows_ref).astype(BF16)
    out_ref[...] = jnp.broadcast_to(rows[None], out_ref.shape)


def own_kernel(
    q_ref, sel_ref, ck_ref, cv_ref, nk_ref, nv_ref, pos_ref, bias_ref, out_ref, log_ref, rows_ref
):
    rows = item_rows(q_ref, rows_ref)
    slots = ck_ref.shape[0]
    scores = dot_t(rows.astype(BF16), ck_ref[...]) * SCALE
    alive = iota((ITEM, slots), 1) < pos_ref[0]
    scores = jnp.where(alive, scores, NEGATIVE)
    top = jnp.max(scores, axis=1, keepdims=True)
    step = iota((ITEM, 1), 0) // PER
    new_scores = []
    for token in range(STEPS):
        key = nk_ref[token : token + 1, :].astype(F32)
        score = jnp.sum(rows * key, axis=1, keepdims=True) * SCALE
        score = jnp.where(step >= token, score, NEGATIVE)
        new_scores.append(score)
        top = jnp.maximum(top, score)
    weights = jnp.where(alive, jnp.exp2(scores - top), 0.0)
    mass = jnp.sum(weights, axis=1, keepdims=True)
    total = dot(weights.astype(BF16), cv_ref[...])
    for token in range(STEPS):
        weight = jnp.where(step >= token, jnp.exp2(new_scores[token] - top), 0.0)
        mass = mass + weight
        value = nv_ref[token : token + 1, :].astype(F32)
        total = total + weight.astype(BF16).astype(F32) * value
    out_ref[...] = total / mass
    log_mass = jnp.broadcast_to(top + jnp.log2(mass), (ITEM, HD))
    log_ref[...] = jnp.broadcast_to(to_lanes(log_mass, 1), log_ref.shape)
    slot_count, samples = sel_ref.shape
    tokens = bias_ref.shape[1]
    blocks = tokens // BLOCK
    number = iota((blocks, samples), 0)
    chosen = jnp.zeros((blocks, samples), F32)
    for slot in range(slot_count):
        chosen = jnp.where(sel_ref[slot : slot + 1, :] == number, 1.0, chosen)
    widen = (iota((blocks, tokens), 1) // BLOCK == iota((blocks, tokens), 0)).astype(F32)
    hit = lax.dot_general(chosen, widen, (((0,), (0,)), ((), ())), preferred_element_type=F32)
    bias_ref[...] = jnp.where(hit > 0.5, 0.0, NEGATIVE)


def prompt_kernel(q_ref, k_ref, v_ref, bias_ref, out_ref):
    samples = q_ref.shape[0]
    tokens = k_ref.shape[0]
    keys = k_ref[...]
    values = jnp.concatenate([v_ref[...], jnp.ones((tokens, HD), BF16)], axis=1)
    for first in range(0, samples, TILE):
        here = slice(first, first + TILE)
        q = q_ref[here].reshape(TILE * ITEM, HD)
        scores = dot_t(q, keys) * SCALE
        scores = scores.reshape(TILE, ITEM, tokens) + bias_ref[here][:, None, :]
        scores = scores.reshape(TILE * ITEM, tokens)
        top = jnp.max(scores, axis=1, keepdims=True)
        weights = jnp.exp2(scores - top).astype(BF16)
        total = dot(weights, values)
        mass = total[:, HD:]
        out_ref[here, :ITEM, :] = (total[:, :HD] / mass).astype(BF16).reshape(TILE, ITEM, HD)
        log_mass = to_lanes(top + jnp.log2(mass), TILE)
        high = log_mass.astype(BF16).astype(F32)
        rest = log_mass - high
        middle = rest.astype(BF16).astype(F32)
        low = rest - middle
        shape = (TILE, STAT, HD)
        row = iota(shape, 1)
        stat = jnp.where(row == 0, jnp.broadcast_to(high[:, None, :], shape), 0.0)
        stat = jnp.where(row == 1, jnp.broadcast_to(middle[:, None, :], shape), stat)
        stat = jnp.where(row == 2, jnp.broadcast_to(low[:, None, :], shape), stat)
        out_ref[here, ITEM:, :] = stat.astype(BF16)


def combine_kernel(part_ref, own_ref, own_log_ref, out_ref):
    shards = part_ref.shape[0]
    log_mass = jnp.sum(part_ref[:, ITEM:, :].astype(F32), axis=1)
    own_log = own_log_ref[0:1, :]
    best = jnp.maximum(jnp.max(log_mass, axis=0, keepdims=True), own_log)
    weights = jnp.exp2(log_mass - best)
    own_weight = jnp.exp2(own_log - best)
    whole = jnp.sum(weights, axis=0, keepdims=True) + own_weight
    weights = weights / whole
    own_weight = own_weight / whole
    per_lane = HD // ITEM
    groups = shards // per_lane
    lane = iota((groups, HD), 1) // ITEM
    packed = jnp.zeros((groups, HD), F32)
    for turn in range(per_lane):
        packed = jnp.where(lane == turn, weights[turn * groups : (turn + 1) * groups], packed)
    pick = iota((ITEM, HD), 0) == iota((ITEM, HD), 1) % ITEM
    factors = []
    rows = []
    for group in range(groups):
        factors.append(jnp.where(pick, packed[group : group + 1], 0.0))
        for turn in range(per_lane):
            rows.append(part_ref[group + turn * groups, :ITEM, :])
    factor = jnp.concatenate(factors, axis=1)
    high = factor.astype(BF16)
    low = (factor - high.astype(F32)).astype(BF16)
    total = dot(jnp.concatenate([high, low], axis=0), jnp.concatenate(rows, axis=0))
    total = total[:ITEM] + total[ITEM:]
    own_column = jnp.sum(
        jnp.where(iota((ITEM, HD), 0) == iota((ITEM, HD), 1), own_weight, 0.0),
        axis=1,
        keepdims=True,
    )
    attended = (total + own_column * own_ref[...]).astype(BF16)
    out_ref[...] = jnp.broadcast_to(attended[None], out_ref.shape)


def project_kernel(x_ref, w_ref, out_ref, rows_ref):
    samples = x_ref.shape[0]
    parts = out_ref.shape[0]
    per_part = samples // parts
    rows_ref[...] = x_ref[...].reshape(samples * ITEM, HD).astype(F32)
    columns = []
    for head in range(PER):
        pieces = [
            rows_ref[pl.ds(step * PER + head, samples, stride=ITEM), :] for step in range(STEPS)
        ]
        columns.append(jnp.concatenate(pieces, axis=0).astype(BF16))
    product = dot(jnp.concatenate(columns, axis=1), w_ref[...])
    for part in range(parts):
        pieces = [
            product[step * samples + part * per_part : step * samples + (part + 1) * per_part]
            for step in range(STEPS)
        ]
        out_ref[part] = jnp.concatenate(pieces, axis=0).astype(out_ref.dtype)


def sum_kernel(x_ref, out_ref):
    total = jnp.sum(x_ref[...].astype(F32), axis=0)
    out_ref[...] = total.reshape(out_ref.shape).astype(BF16)


def call(kernel, name, out_shape, in_specs, out_specs, scratch=(), flops=0, moved=0):
    return pl.pallas_call(
        kernel,
        name=name,
        out_shape=out_shape,
        in_specs=in_specs,
        out_specs=out_specs,
        scratch_shapes=scratch,
        compiler_params=PARAMS,
        cost_estimate=pl.CostEstimate(flops=flops, bytes_accessed=moved, transcendentals=0),
    )


def swap(array, axis):
    return lax.all_to_all(array, axis, split_axis=0, concat_axis=0, tiled=True)


def shards(
    queries,
    prompt_keys,
    prompt_values,
    selected,
    cache_keys,
    cache_values,
    new_keys,
    new_values,
    positions,
    out_weight,
):
    samples = lax.axis_size("ctx")
    parts = lax.axis_size("head")
    tokens = prompt_keys.shape[0]
    columns = out_weight.shape[1]
    struct = jax.ShapeDtypeStruct
    rows_scratch = pltpu.VMEM((ITEM, HD), F32)
    q = queries.reshape(STEPS, PER * HD)
    spread = call(
        spread_kernel, "spread", struct((samples, ITEM, HD), BF16), [VMEM], VMEM, [rows_scratch]
    )(q)
    gathered = swap(spread, "ctx")
    bias, own, own_log = call(
        own_kernel,
        "own",
        (struct((samples, tokens), F32), struct((ITEM, HD), F32), struct((8, HD), F32)),
        [VMEM] * 6 + [SMEM],
        (VMEM, VMEM, VMEM),
        [rows_scratch],
        flops=10**6,
        moved=3 * 10**5,
    )(
        q,
        selected[:, 0, :].T,
        cache_keys[0],
        cache_values[0],
        new_keys[:, 0],
        new_values[:, 0],
        positions,
    )
    parts_out = call(
        prompt_kernel,
        "prompt",
        struct((samples, ITEM + STAT, HD), BF16),
        [VMEM] * 4,
        VMEM,
    )(gathered, prompt_keys, prompt_values, bias)
    received = swap(parts_out, "ctx")
    attended = call(
        combine_kernel, "combine", struct((samples, ITEM, HD), BF16), [VMEM] * 3, VMEM
    )(received, own, own_log)
    every = swap(attended, "ctx")
    product = call(
        project_kernel,
        "project",
        struct((parts, STEPS * samples // parts, columns), F32),
        [VMEM] * 2,
        VMEM,
        [pltpu.VMEM((samples * ITEM, HD), F32)],
    )(every, out_weight)
    terms = swap(product, "head")
    return call(
        sum_kernel, "sum", struct((STEPS, samples // parts, columns), BF16), [VMEM], VMEM
    )(terms)


def solution(mesh):
    placed = (
        P(None, "ctx", "head"),
        P("ctx", "head"),
        P("ctx", "head"),
        P(None, "head", "ctx"),
        P("ctx", None, "head"),
        P("ctx", None, "head"),
        P(None, "ctx", "head"),
        P(None, "ctx", "head"),
        P("ctx"),
        P("head", "ctx"),
    )
    return jax.shard_map(
        shards, mesh=mesh, in_specs=placed, out_specs=P(None, "head", "ctx"), check_vma=False
    )
```

time: 274 us -> 102 us (0.37)
  waiting for transfers between devices: 93.4 us -> 16 us
  blocking collectives: 125 us -> 62.7 us
  between operations: 14.3 us -> 0.81 us
  other arithmetic: 9.32 us -> 0 us
  local copies, waits for them, and re-layouts: 9.61 us -> 0.74 us
  matrix products: 4.76 us -> 0 us
  Pallas kernels: 0 us -> 4.63 us
    all_gather x3 -> x0, blocking collectives: 125 us -> none  [the longest x2 81.7 us: shards(): lax.all_gather(queries[step_index:step_index + 1], 'ctx', axis=1, tiled=T...]
    all_to_all x0 -> x3, blocking collectives: none -> 62.7 us  [swap(): return lax.all_to_all(array, axis, split_axis=0, concat_axis=0, tiled=True)]
    reduce_scatter x1 -> x0, waiting for transfers between devices: 62.3 us -> none  [shards(): mixed = lax.psum_scatter(terms, 'head', scatter_dimension=1, tiled=True)]
    all_to_all x3 -> x1, waiting for transfers between devices: 31.1 us -> 16 us  [swap(): return lax.all_to_all(array, axis, split_axis=0, concat_axis=0, tiled=True)]
    dot_general x13 -> x0, matrix products: 4.76 us -> none  [the longest x4 1.58 us: one_block(): jnp.einsum('srgqd,tgd->srgqt', query_part, key_rows, preferred_element_ty...]
    pallas_call x0 -> x6, Pallas kernels: none -> 4.63 us  [the longest x1 1.61 us: shards(): call(prompt_kernel, 'prompt', struct((samples, ITEM + STAT, HD), BF16), [...]
    mul x6 -> x0, local copies, waits for them, and re-layouts: 3.3 us -> none  [the longest x2 3.13 us: shards(): factor[..., None] * widened]
    all_gather x2 -> x0, other arithmetic: 3.02 us -> none  [shards(): lax.all_gather(queries[step_index:step_index + 1], 'ctx', axis=1, tiled=T...]
  transfers between devices with their start and end apart: 4 -> 1, of which waited for: 4 -> 1; matrix products, arithmetic and copies ran while one was open for 3% -> 0% of each run, Pallas kernels for 0% -> 0%
where the time goes in v1:
time: 102 us
  blocking collectives  62.7 us (61%)
  starting transfers between devices  17.3 us (17%)
  waiting for transfers between devices  16 us (16%)
  Pallas kernels  4.63 us (5%)
    all_to_all x3, blocking collectives, swap(): return lax.all_to_all(array, axis, split_axis=0, concat_axis=0, tiled=True)  62.7 us
    all_to_all x1, starting transfers between devices, swap(): return lax.all_to_all(array, axis, split_axis=0, concat_axis=0, tiled=True)  17.3 us
    all_to_all x1, waiting for transfers between devices, swap(): return lax.all_to_all(array, axis, split_axis=0, concat_axis=0, tiled=True)  16 us
  transfers between devices with their start and end apart: 1, of which 1 were waited for; matrix products, arithmetic and copies ran while one was open for 0% of the time, Pallas kernels for 0%

profile of v1, /device:TPU:1, one launch (start us, length us, event | category | flops | bytes accessed | tf_op | source)
XLA Modules:
  0.0 102.1 jit_solution(14453079227368027971)
XLA Ops:
  0.0 0.0 copy-start.5
  0.0 0.7 copy-done.5
  0.7 0.9 spread.1
  1.6 0.0 copy-start.3
  1.6 0.0 copy-start.4
  1.6 0.0 copy-start.6
  1.6 0.0 copy-start.7
  1.6 0.0 copy-start.8
  1.6 0.0 copy-start.9
  1.6 0.0 copy-start.2
  1.6 17.3 %all-to-all-start = ((bf16[64,32,128]{2,1,0:T(8,128)(2,1)}), bf16[64,32,128]{2,1,0:T(8,128)(2,1)S(1)}, u32[]{:S(2)}, u32[]{:S(2)}) async-start(bf16[64,32,128]{2,1,0:T(8,128)(2,1)} %spread.1), calls=%async_computation | async-start | bytes 1048576 | tf_op jit(solution)/shard_map/all_to_all | solution.py:204
  18.9 0.0 copy-start.1
  19.6 0.0 copy-done.3
  19.6 0.0 copy-done.4
  19.6 0.0 copy-done.6
  19.6 0.0 copy-done.7
  19.6 0.0 copy-done.8
  19.6 0.0 copy-done.9
  19.6 0.4 own.1
  20.0 16.0 %all-to-all-done.q_ref = bf16[64,32,128]{2,1,0:T(8,128)(2,1)S(1)} async-done(((bf16[64,32,128]{2,1,0:T(8,128)(2,1)}), bf16[64,32,128]{2,1,0:T(8,128)(2,1)S(1)}, u32[]{:S(2)}, u32[]{:S(2)}) %all-to-all-start) | async-done | bytes 524320 | tf_op jit(solution)/shard_map/all_to_all | solution.py:204
  36.1 0.0 copy-done.2
  36.1 0.0 copy-done.1
  36.1 1.6 %prompt.1 = bf16[64,40,128]{2,1,0:T(8,128)(2,1)S(1)} custom-call(bf16[64,32,128]{2,1,0:T(8,128)(2,1)S(1)} %all-to-all-done.q_ref, bf16[512,128]{1,0:T(8,128)(2,1)S(1)} %copy-done.1, bf16[512,128]{1,0:T(8,128)(2,1)S(1)} %copy-done.2, f32[64,512]{1,0:T(8,128)S(1)} %get-tuple-element.8.bias_ref), custom_call_target="tpu_custom_call" | custom-call | tf_op jit(solution)/shard_map/prompt/pallas_call | solution.py:248
  37.7 24.9 %all_to_all.20.part_ref = bf16[64,40,128]{2,1,0:T(8,128)(2,1)S(1)} all-to-all(bf16[64,40,128]{2,1,0:T(8,128)(2,1)S(1)} %prompt.1), channel_id=1, replica_groups=mesh['ctx'=64,'head'=8] {'ctx'}, dimensions={0} | all-to-all | bytes 1310720 | tf_op jit(solution)/shard_map/all_to_all | solution.py:204
  62.6 0.0 copy-start
  62.6 0.4 combine.1
  63.0 23.2 %all_to_all.21.x_ref = bf16[64,32,128]{2,1,0:T(8,128)(2,1)S(1)} all-to-all(bf16[64,32,128]{2,1,0:T(8,128)(2,1)S(1)} %combine.1), channel_id=1, replica_groups=mesh['ctx'=64,'head'=8] {'ctx'}, dimensions={0} | all-to-all | bytes 1048576 | tf_op jit(solution)/shard_map/all_to_all | solution.py:204
  86.2 0.0 copy-done
  86.2 0.8 project.1
  87.0 14.5 %all_to_all.22.x_ref = f32[8,16,256]{2,1,0:T(8,128)S(1)} all-to-all(f32[8,16,256]{2,1,0:T(8,128)S(1)} %project.1), channel_id=1, replica_groups=mesh['ctx'=64,'head'=8] {'head'}, dimensions={0} | all-to-all | bytes 262144 | tf_op jit(solution)/shard_map/all_to_all | solution.py:204
  101.5 0.6 sum.1
Async XLA Ops:
  0.0 0.7 copy-start.5
  1.6 18.0 %copy-start.3 = (bf16[1,256,128]{2,1,0:T(8,128)(2,1)S(1)}, bf16[1,256,128]{2,1,0:T(8,128)(2,1)}, u32[]{:S(2)}) copy-start(bf16[1,256,128]{2,1,0:T(8,128)(2,1)} %param.14) | copy-start | bytes 196612
  1.6 18.0 %copy-start.4 = (bf16[1,256,128]{2,1,0:T(8,128)(2,1)S(1)}, bf16[1,256,128]{2,1,0:T(8,128)(2,1)}, u32[]{:S(2)}) copy-start(bf16[1,256,128]{2,1,0:T(8,128)(2,1)} %param.15) | copy-start | bytes 196612
  1.6 18.0 %copy-start.6 = (bf16[2,1,2048]{2,0,1:T(2,128)(2,1)S(1)}, bf16[2,1,2048]{2,0,1:T(2,128)(2,1)}, u32[]{:S(2)}) copy-start(bf16[2,1,2048]{2,0,1:T(2,128)(2,1)} %param.10) | copy-start | bytes 24580
  1.6 18.1 %copy-start.7 = (s32[64,1,8]{0,2,1:T(8,128)S(1)}, s32[64,1,8]{0,2,1:T(8,128)}, u32[]{:S(2)}) copy-start(s32[64,1,8]{0,2,1:T(8,128)} %param.13) | copy-start | bytes 6148
  1.6 18.1 %copy-start.8 = (bf16[2,1,128]{2,0,1:T(2,128)(2,1)S(1)}, bf16[2,1,128]{2,0,1:T(2,128)(2,1)}, u32[]{:S(2)}) copy-start(bf16[2,1,128]{2,0,1:T(2,128)(2,1)} %param.16) | copy-start | bytes 1540
  1.6 18.1 %copy-start.9 = (bf16[2,1,128]{2,0,1:T(2,128)(2,1)S(1)}, bf16[2,1,128]{2,0,1:T(2,128)(2,1)}, u32[]{:S(2)}) copy-start(bf16[2,1,128]{2,0,1:T(2,128)(2,1)} %param.17) | copy-start | bytes 1540
  1.6 34.5 %copy-start.2 = (bf16[512,128]{1,0:T(8,128)(2,1)S(1)}, bf16[512,128]{1,0:T(8,128)(2,1)}, u32[]{:S(2)}) copy-start(bf16[512,128]{1,0:T(8,128)(2,1)} %v_ref.1) | copy-start | bytes 393220
  1.6 34.5 %all-to-all-start = ((bf16[64,32,128]{2,1,0:T(8,128)(2,1)}), bf16[64,32,128]{2,1,0:T(8,128)(2,1)S(1)}, u32[]{:S(2)}, u32[]{:S(2)}) async-start(bf16[64,32,128]{2,1,0:T(8,128)(2,1)} %spread.1), calls=%async_computation | async-start | bytes 1048576 | tf_op jit(solution)/shard_map/all_to_all | solution.py:204
  18.9 17.2 %copy-start.1 = (bf16[512,128]{1,0:T(8,128)(2,1)S(1)}, bf16[512,128]{1,0:T(8,128)(2,1)}, u32[]{:S(2)}) copy-start(bf16[512,128]{1,0:T(8,128)(2,1)} %k_ref.1) | copy-start | bytes 393220
  62.6 23.6 %copy-start = (bf16[2048,256]{1,0:T(8,128)(2,1)S(1)}, bf16[2048,256]{1,0:T(8,128)(2,1)}, u32[]{:S(2)}) copy-start(bf16[2048,256]{1,0:T(8,128)(2,1)} %w_ref.1) | copy-start | bytes 3145732

commit v2 on v1

v2 whole, which is shorter than its diff:
```python
import math

import jax
import jax.numpy as jnp
from jax import lax
from jax.experimental import pallas as pl
from jax.experimental.pallas import tpu as pltpu
from jax.sharding import Mesh
from jax.sharding import PartitionSpec as P

HD = 128
PER = 16
BLOCK = 64
STEPS = 2
HALVES = 2
HALF = PER // HALVES
PART = STEPS * HALF
ITEM = HALVES * PART
STAT = 8
FLAG = 16
NEGATIVE = -1e30
SCALE = math.log2(math.e) / math.sqrt(HD)
TILE = 8
SAMPLES = ("zh", "zl", "yh")

VMEM = pl.BlockSpec(memory_space=pltpu.VMEM)
SMEM = pl.BlockSpec(memory_space=pltpu.SMEM)
PARAMS = pltpu.CompilerParams(vmem_limit_bytes=24 * 1024 * 1024)
F32 = jnp.float32
BF16 = jnp.bfloat16


def dot(a, b):
    return lax.dot_general(a, b, (((1,), (0,)), ((), ())), preferred_element_type=F32)


def dot_t(a, b):
    return lax.dot_general(a, b, (((1,), (1,)), ((), ())), preferred_element_type=F32)


def iota(shape, dim):
    return lax.broadcasted_iota(jnp.int32, shape, dim)


def item_rows(q_ref, rows_ref):
    whole = q_ref[...].astype(F32)
    for step in range(STEPS):
        for head in range(PER):
            row = head // HALF * PART + step * HALF + head % HALF
            rows_ref[row : row + 1, :] = whole[step : step + 1, head * HD : (head + 1) * HD]
    return rows_ref[...]


def spread_kernel(q_ref, out_ref, rows_ref):
    rows = item_rows(q_ref, rows_ref).astype(BF16)
    out_ref[...] = jnp.broadcast_to(rows[None], out_ref.shape)


def pack_kernel(k_ref, v_ref, sel_ref, out_ref):
    tokens = k_ref.shape[0]
    out_ref[:tokens, :] = k_ref[...]
    out_ref[tokens : 2 * tokens, :] = v_ref[...]
    slots, samples = sel_ref.shape
    number = iota((FLAG, samples), 0)
    chosen = jnp.zeros((FLAG, samples), F32)
    for slot in range(slots):
        chosen = jnp.where(sel_ref[slot : slot + 1, :] == number, 1.0, chosen)
    chosen = jnp.concatenate([chosen, jnp.zeros((FLAG, HD - samples), F32)], axis=1)
    out_ref[2 * tokens :, :] = chosen.astype(BF16)


def own_kernel(q_ref, ck_ref, cv_ref, nk_ref, nv_ref, pos_ref, out_ref, log_ref, rows_ref):
    rows = item_rows(q_ref, rows_ref)
    slots = ck_ref.shape[0]
    scores = dot_t(rows.astype(BF16), ck_ref[...]) * SCALE
    alive = iota((ITEM, slots), 1) < pos_ref[0]
    scores = jnp.where(alive, scores, NEGATIVE)
    top = jnp.max(scores, axis=1, keepdims=True)
    step = iota((ITEM, 1), 0) // HALF % STEPS
    new_scores = []
    for token in range(STEPS):
        key = nk_ref[token : token + 1, :].astype(F32)
        score = jnp.sum(rows * key, axis=1, keepdims=True) * SCALE
        score = jnp.where(step >= token, score, NEGATIVE)
        new_scores.append(score)
        top = jnp.maximum(top, score)
    weights = jnp.where(alive, jnp.exp2(scores - top), 0.0)
    mass = jnp.sum(weights, axis=1, keepdims=True)
    total = dot(weights.astype(BF16), cv_ref[...])
    for token in range(STEPS):
        weight = jnp.where(step >= token, jnp.exp2(new_scores[token] - top), 0.0)
        mass = mass + weight
        value = nv_ref[token : token + 1, :].astype(F32)
        total = total + weight.astype(BF16).astype(F32) * value
    out_ref[...] = total / mass
    log_ref[...] = jnp.broadcast_to(top + jnp.log2(mass), (ITEM, HD))


def bias_of(pack_ref, yl, samples, tokens):
    flags = pack_ref[2 * tokens :, :]
    mine = (iota((samples, HD), 1) == 2 * iota((samples, HD), 0) + yl).astype(BF16)
    chosen = dot_t(mine, flags).astype(BF16)
    widen = iota((FLAG, tokens), 1) // BLOCK == iota((FLAG, tokens), 0)
    hit = dot(chosen, widen.astype(BF16))
    return jnp.where(hit > 0.5, 0.0, NEGATIVE)


def prompt_kernel(
    place_ref, q_ref, here_ref, there_ref, own_ref, own_log_ref, out_ref, total_ref, log_ref
):
    samples = q_ref.shape[0]
    tokens = (here_ref.shape[0] - FLAG) // 2
    packs = (here_ref, there_ref)
    bias = jnp.concatenate(
        [bias_of(ref, place_ref[1], samples, tokens) for ref in packs], axis=1
    )
    keys = jnp.concatenate([ref[:tokens, :] for ref in packs], axis=0)
    values = jnp.concatenate([ref[tokens : 2 * tokens, :] for ref in packs], axis=0)
    values = jnp.concatenate([values, jnp.ones((2 * tokens, HD), BF16)], axis=1)
    for first in range(0, samples, TILE):
        here = slice(first, first + TILE)
        rows = slice(first * ITEM, (first + TILE) * ITEM)
        q = q_ref[here].reshape(TILE * ITEM, HD)
        scores = dot_t(q, keys) * SCALE
        scores = scores.reshape(TILE, ITEM, 2 * tokens) + bias[here][:, None, :]
        scores = scores.reshape(TILE * ITEM, 2 * tokens)
        top = jnp.max(scores, axis=1, keepdims=True)
        weights = jnp.exp2(scores - top).astype(BF16)
        total = dot(weights, values)
        mass = total[:, HD:]
        total_ref[rows, :] = total[:, :HD] / mass
        log_ref[rows, :] = top + jnp.log2(mass)
    mine = pl.ds(pl.multiple_of(place_ref[0] * ITEM, ITEM), ITEM)
    log = log_ref[mine, :]
    own_log = own_log_ref[...]
    best = jnp.maximum(log, own_log)
    factor = jnp.exp2(log - best)
    own_factor = jnp.exp2(own_log - best)
    mass = factor + own_factor
    total_ref[mine, :] = (total_ref[mine, :] * factor + own_ref[...] * own_factor) / mass
    log_ref[mine, :] = best + jnp.log2(mass)
    shape = (ITEM, HD)
    pick = iota(shape, 0) == iota(shape, 1) % ITEM
    row = iota((STAT, HD), 0)
    inner = samples // 8
    for outer in range(samples // (HALVES * inner)):
        for half in range(HALVES):
            for last in range(inner):
                target = (outer * HALVES + half) * inner + last
                slices = []
                for turn in range(HALVES):
                    start = ((outer * HALVES + turn) * inner + last) * ITEM + half * PART
                    slices.append(slice(start, start + PART))
                part = jnp.concatenate([total_ref[rows, :] for rows in slices], axis=0)
                out_ref[target, :ITEM, :] = part.astype(BF16)
                log = jnp.concatenate([log_ref[rows, :] for rows in slices], axis=0)
                log = jnp.sum(jnp.where(pick, log, 0.0), axis=0, keepdims=True)
                high = log.astype(BF16).astype(F32)
                rest = log - high
                middle = rest.astype(BF16).astype(F32)
                low = rest - middle
                stat = jnp.where(row == 1, middle, jnp.where(row == 2, low, 0.0))
                stat = jnp.where(row == 0, high, stat)
                out_ref[target, ITEM:, :] = stat.astype(BF16)


def combine_kernel(part_ref, out_ref):
    shards = part_ref.shape[0]
    log_mass = jnp.sum(part_ref[:, ITEM:, :].astype(F32), axis=1)
    weights = jnp.exp2(log_mass - jnp.max(log_mass, axis=0, keepdims=True))
    weights = weights / jnp.sum(weights, axis=0, keepdims=True)
    per_lane = HD // ITEM
    groups = shards // per_lane
    lane = iota((groups, HD), 1) // ITEM
    packed = jnp.zeros((groups, HD), F32)
    for turn in range(per_lane):
        packed = jnp.where(lane == turn, weights[turn * groups : (turn + 1) * groups], packed)
    pick = iota((ITEM, HD), 0) == iota((ITEM, HD), 1) % ITEM
    factors = []
    rows = []
    for group in range(groups):
        factors.append(jnp.where(pick, packed[group : group + 1], 0.0))
        for turn in range(per_lane):
            rows.append(part_ref[group + turn * groups, :ITEM, :])
    factor = jnp.concatenate(factors, axis=1)
    high = factor.astype(BF16)
    low = (factor - high.astype(F32)).astype(BF16)
    total = dot(jnp.concatenate([high, low], axis=0), jnp.concatenate(rows, axis=0))
    attended = (total[:ITEM] + total[ITEM:]).astype(BF16)
    out_ref[...] = jnp.broadcast_to(attended[None], out_ref.shape)


def project_kernel(place_ref, x_ref, w_ref, other_ref, out_ref, rows_ref):
    peers = x_ref.shape[0]
    depth = HALF * HD
    rows_ref[...] = x_ref[...].reshape(peers * ITEM, HD).astype(F32)
    columns = []
    for head in range(HALF):
        pieces = [
            rows_ref[pl.ds(turn * PART + step * HALF + head, peers, stride=ITEM), :]
            for turn in range(HALVES)
            for step in range(STEPS)
        ]
        columns.append(jnp.concatenate(pieces, axis=0).astype(BF16))
    left = jnp.concatenate(columns, axis=1)
    half = place_ref[2]
    mine = pl.ds(pl.multiple_of(half * depth, depth), depth)
    parts = out_ref.shape[0] // HALVES
    outer = parts // HALVES
    for owner, weight in ((half, w_ref[mine, :]), (1 - half, other_ref[...])):
        product = dot(left, weight)
        for part in range(parts):
            first, turn = part // HALVES, part % HALVES
            size = peers // outer
            pieces = []
            for step in range(STEPS):
                start = (turn * STEPS + step) * peers + first * size
                pieces.append(product[start : start + size])
            out_ref[owner * parts + part] = jnp.concatenate(pieces, axis=0).astype(BF16)


def sum_kernel(x_ref, out_ref):
    total = jnp.sum(x_ref[...].astype(F32), axis=0)
    out_ref[...] = total.reshape(out_ref.shape).astype(BF16)


def call(kernel, name, out_shape, in_specs, out_specs, scratch=(), flops=0, moved=0):
    return pl.pallas_call(
        kernel,
        name=name,
        out_shape=out_shape,
        in_specs=in_specs,
        out_specs=out_specs,
        scratch_shapes=scratch,
        compiler_params=PARAMS,
        cost_estimate=pl.CostEstimate(flops=flops, bytes_accessed=moved, transcendentals=0),
    )


def swap(array, axes):
    return lax.all_to_all(array, axes, split_axis=0, concat_axis=0, tiled=True)


def shards(
    queries,
    prompt_keys,
    prompt_values,
    selected,
    cache_keys,
    cache_values,
    new_keys,
    new_values,
    positions,
    out_weight,
):
    struct = jax.ShapeDtypeStruct
    samples = lax.axis_size(SAMPLES)
    heads = lax.axis_size("head")
    tokens = prompt_keys.shape[0]
    depth, columns = HALF * HD, out_weight.shape[1]
    half = lax.axis_index("zl")
    place = jnp.stack([lax.axis_index(SAMPLES), lax.axis_index("yl"), half]).astype(jnp.int32)
    rows_scratch = pltpu.VMEM((ITEM, HD), F32)
    q = queries.reshape(STEPS, PER * HD)
    pair = [(0, 1), (1, 0)]

    spread = call(
        spread_kernel, "spread", struct((samples, ITEM, HD), BF16), [VMEM], VMEM, [rows_scratch]
    )(q)
    here = call(
        pack_kernel, "pack", struct((2 * tokens + FLAG, HD), BF16), [VMEM] * 3, VMEM
    )(prompt_keys, prompt_values, selected[:, 0, :].T)
    gathered = swap(spread, SAMPLES)
    there = lax.ppermute(here, "yl", pair)
    other_weight = lax.ppermute(
        lax.dynamic_slice_in_dim(out_weight, (1 - half) * depth, depth, axis=0), "zl", pair
    )
    own, own_log = call(
        own_kernel,
        "own",
        (struct((ITEM, HD), F32), struct((ITEM, HD), F32)),
        [VMEM] * 5 + [SMEM],
        (VMEM, VMEM),
        [rows_scratch],
        flops=10**6,
        moved=3 * 10**5,
    )(q, cache_keys[0], cache_values[0], new_keys[:, 0], new_values[:, 0], positions)
    partial = call(
        prompt_kernel,
        "prompt",
        struct((samples, ITEM + STAT, HD), BF16),
        [SMEM] + [VMEM] * 5,
        VMEM,
        [pltpu.VMEM((samples * ITEM, HD), F32)] * 2,
    )(place, gathered, here, there, own, own_log)
    received = swap(partial, SAMPLES)
    attended = call(
        combine_kernel, "combine", struct((samples, ITEM, HD), BF16), [VMEM], VMEM
    )(received)
    every = swap(attended, ("zh", "yh", "yl"))
    product = call(
        project_kernel,
        "project",
        struct((HALVES * heads, STEPS * 2 * samples // heads, columns), BF16),
        [SMEM] + [VMEM] * 3,
        VMEM,
        [pltpu.VMEM((samples * ITEM, HD), F32)],
    )(place, every, out_weight, other_weight)
    terms = swap(product, ("zl", "head"))
    return call(
        sum_kernel, "sum", struct((STEPS, 2 * samples // heads, columns), BF16), [VMEM], VMEM
    )(terms)


def solution(mesh):
    fine = Mesh(mesh.devices.reshape(4, 2, 4, 2, 8), ("zh", "zl", "yh", "yl", "head"))
    ctx = ("zh", "zl", "yh", "yl")
    placed = (
        P(None, ctx, "head"),
        P(ctx, "head"),
        P(ctx, "head"),
        P(None, "head", ctx),
        P(ctx, None, "head"),
        P(ctx, None, "head"),
        P(None, ctx, "head"),
        P(None, ctx, "head"),
        P(ctx),
        P("head", ctx),
    )
    return jax.shard_map(
        shards, mesh=fine, in_specs=placed, out_specs=P(None, "head", ctx), check_vma=False
    )
```

time: 102 us -> 95.3 us (0.934)
  blocking collectives: 62.7 us -> 14.6 us
  starting transfers between devices: 17.3 us -> 39.8 us
  waiting for transfers between devices: 16 us -> 31.6 us
  Pallas kernels: 4.63 us -> 7.11 us
    all_to_all x3 -> x1, blocking collectives: 62.7 us -> 14.6 us  [swap(): return lax.all_to_all(array, axes, split_axis=0, concat_axis=0, tiled=True)]
    all_to_all x1 -> x3, starting transfers between devices: 17.3 us -> 34.2 us  [swap(): return lax.all_to_all(array, axes, split_axis=0, concat_axis=0, tiled=True)]
    ppermute x0 -> x2, waiting for transfers between devices: none -> 9.29 us  [the longest x1 8.89 us: shards(): there = lax.ppermute(here, 'yl', pair)]
    all_to_all x1 -> x3, waiting for transfers between devices: 16 us -> 22.3 us  [swap(): return lax.all_to_all(array, axes, split_axis=0, concat_axis=0, tiled=True)]
    ppermute x0 -> x2, starting transfers between devices: none -> 5.58 us  [the longest x1 3.14 us: shards(): lax.ppermute(lax.dynamic_slice_in_dim(out_weight, (1 - half) * depth, dep...]
    pallas_call x1, Pallas kernels: 1.61 us -> 3.38 us  [shards(): call(prompt_kernel, 'prompt', struct((samples, ITEM + STAT, HD), BF16), [...]
  transfers between devices with their start and end apart: 1 -> 5, of which waited for: 1 -> 4; matrix products, arithmetic and copies ran while one was open for 0% -> 0% of each run, Pallas kernels for 0% -> 1%
where the time goes in v2:
time: 95.3 us; the launch traced here: 94.7 us
  starting transfers between devices  39.8 us (42%)
  waiting for transfers between devices  31.6 us (33%)
  blocking collectives  14.6 us (15%)
  Pallas kernels  7.11 us (7%)
    all_to_all x3, starting transfers between devices, swap(): return lax.all_to_all(array, axes, split_axis=0, concat_axis=0, tiled=True)  34.2 us
    all_to_all x3, waiting for transfers between devices, swap(): return lax.all_to_all(array, axes, split_axis=0, concat_axis=0, tiled=True)  22.3 us
    all_to_all x1, blocking collectives, swap(): return lax.all_to_all(array, axes, split_axis=0, concat_axis=0, tiled=True)  14.6 us
    ppermute x1, waiting for transfers between devices, shards(): there = lax.ppermute(here, 'yl', pair)  8.89 us
    pallas_call x1, Pallas kernels, shards(): call(prompt_kernel, 'prompt', struct((samples, ITEM + STAT, HD), BF16), [...  3.38 us
    ppermute x1, starting transfers between devices, shards(): lax.ppermute(lax.dynamic_slice_in_dim(out_weight, (1 - half) * depth, dep...  3.14 us
    ppermute x1, starting transfers between devices, shards(): there = lax.ppermute(here, 'yl', pair)  2.44 us
  transfers between devices with their start and end apart: 5, of which 4 were waited for; matrix products, arithmetic and copies ran while one was open for 0% of the time, Pallas kernels for 1%

profile of v2, /device:TPU:1, one launch (start us, length us, event | category | flops | bytes accessed | tf_op | source)
XLA Modules:
  0.0 94.7 jit_solution(15850098961607854301)
XLA Ops:
  0.0 0.0 copy-start.5
  0.0 0.7 copy-done.5
  0.7 0.7 spread.1
  1.4 0.0 copy-start.1
  1.4 0.0 copy-start.2
  1.4 0.0 copy-start.7
  1.4 16.6 %all-to-all-start = ((bf16[32,32,128]{2,1,0:T(8,128)(2,1)}), bf16[32,32,128]{2,1,0:T(8,128)(2,1)S(1)}, u32[]{:S(2)}, u32[]{:S(2)}) async-start(bf16[32,32,128]{2,1,0:T(8,128)(2,1)} %spread.1), calls=%async_computation | async-start | bytes 524288 | tf_op jit(solution)/shard_map/all_to_all | solution.py:241
  18.1 0.0 copy-done.1
  18.1 0.0 copy-done.2
  18.1 0.0 copy-done.7
  18.1 0.0 copy-start.3
  18.1 0.0 copy-start.4
  18.2 0.0 copy-start.6
  18.2 0.0 copy-start.8
  18.2 0.0 copy-start.9
  18.2 0.0 copy-start
  18.2 2.4 %collective-permute-start = (bf16[1040,128]{1,0:T(8,128)(2,1)S(1)}, bf16[1040,128]{1,0:T(8,128)(2,1)S(1)}, u32[]{:S(2)}, u32[]{:S(2)}) collective-permute-start(bf16[1040,128]{1,0:T(8,128)(2,1)S(1)} %pack.1.here_ref), channel_id=1, source_target_pairs={{0,8},{8,0},{1,9},{9,1},{2,10},{10,2},{3,11},{11,3},{4,12},{12,4},... | collective-permute-start | bytes 798728 | tf_op jit(solution)/shard_map/ppermute | solution.py:274
  21.3 0.0 copy-done.3
  21.4 0.0 copy-done.4
  21.4 0.0 copy-done.6
  21.4 0.0 copy-done.8
  21.4 0.0 copy-done.9
  21.4 0.4 own.1
  21.8 0.1 pad_add_fusion.place_ref
  21.8 8.9 %collective-permute-done.there_ref = bf16[1040,128]{1,0:T(8,128)(2,1)S(1)} collective-permute-done((bf16[1040,128]{1,0:T(8,128)(2,1)S(1)}, bf16[1040,128]{1,0:T(8,128)(2,1)S(1)}, u32[]{:S(2)}, u32[]{:S(2)}) %collective-permute-start) | collective-permute-done | bytes 266272 | tf_op jit(solution)/shard_map/ppermute | solution.py:274
  30.7 0.0 all-to-all-done.q_ref
  30.7 3.4 %prompt.1 = bf16[32,40,128]{2,1,0:T(8,128)(2,1)} custom-call(s32[3]{0:T(128)S(1)} %pad_add_fusion.place_ref, bf16[32,32,128]{2,1,0:T(8,128)(2,1)S(1)} %all-to-all-done.q_ref, bf16[1040,128]{1,0:T(8,128)(2,1)S(1)} %pack.1.here_ref, bf16[1040,128]{1,0:T(8,128)(2,1)S(1)} %collective-permute-done.there_ref, f32[32,128]{1,0:T(8,128)S(1)} %get-tuple-element.7.own_ref, ...), custom_call_target="tpu_custom_call" | custom-call | tf_op jit(solution)/shard_map/prompt/pallas_call | solution.py:288
  34.1 11.2 %all-to-all-start.1 = ((bf16[32,40,128]{2,1,0:T(8,128)(2,1)}), bf16[32,40,128]{2,1,0:T(8,128)(2,1)S(1)}, u32[]{:S(2)}, u32[]{:S(2)}) async-start(bf16[32,40,128]{2,1,0:T(8,128)(2,1)} %prompt.1), calls=%async_computation.1 | async-start | bytes 655360 | tf_op jit(solution)/shard_map/all_to_all | solution.py:241
  45.3 0.0 copy-done
  45.4 3.1 %collective-permute-start.1 = (bf16[1024,256]{1,0:T(8,128)(2,1)S(1)}, bf16[1024,256]{1,0:T(8,128)(2,1)S(1)}, u32[]{:S(2)}, u32[]{:S(2)}) collective-permute-start(bf16[1024,256]{1,0:T(8,128)(2,1)S(1)} %constant_dynamic-slice_fusion), channel_id=1, source_target_pairs={{0,64},{64,0},{1,65},{65,1},{2,66},{66,2},{3,67},{67,3},{4,68},{68... | collective-permute-start | bytes 1572872 | tf_op jit(solution)/shard_map/ppermute | solution.py:275
  48.5 10.2 %all-to-all-done.1.part_ref = bf16[32,40,128]{2,1,0:T(8,128)(2,1)S(1)} async-done(((bf16[32,40,128]{2,1,0:T(8,128)(2,1)}), bf16[32,40,128]{2,1,0:T(8,128)(2,1)S(1)}, u32[]{:S(2)}, u32[]{:S(2)}) %all-to-all-start.1) | async-done | bytes 327712 | tf_op jit(solution)/shard_map/all_to_all | solution.py:241
  58.8 1.0 %combine.1 = bf16[32,32,128]{2,1,0:T(8,128)(2,1)} custom-call(bf16[32,40,128]{2,1,0:T(8,128)(2,1)S(1)} %all-to-all-done.1.part_ref), custom_call_target="tpu_custom_call" | custom-call | tf_op jit(solution)/shard_map/combine/pallas_call | solution.py:297
  59.7 6.4 %all-to-all-start.2 = ((bf16[32,32,128]{2,1,0:T(8,128)(2,1)}), bf16[32,32,128]{2,1,0:T(8,128)(2,1)S(1)}, u32[]{:S(2)}, u32[]{:S(2)}) async-start(bf16[32,32,128]{2,1,0:T(8,128)(2,1)} %combine.1), calls=%async_computation.2 | async-start | bytes 524288 | tf_op jit(solution)/shard_map/all_to_all | solution.py:241
  66.1 0.4 collective-permute-done.1.other_ref
  66.5 12.0 %all-to-all-done.2.x_ref = bf16[32,32,128]{2,1,0:T(8,128)(2,1)S(1)} async-done(((bf16[32,32,128]{2,1,0:T(8,128)(2,1)}), bf16[32,32,128]{2,1,0:T(8,128)(2,1)S(1)}, u32[]{:S(2)}, u32[]{:S(2)}) %all-to-all-start.2) | async-done | bytes 262176 | tf_op jit(solution)/shard_map/all_to_all | solution.py:241
  78.5 1.0 %project.1 = bf16[16,16,256]{2,1,0:T(8,128)(2,1)S(1)} custom-call(s32[3]{0:T(128)S(1)} %pad_add_fusion.place_ref, bf16[32,32,128]{2,1,0:T(8,128)(2,1)S(1)} %all-to-all-done.2.x_ref, bf16[2048,256]{1,0:T(8,128)(2,1)S(1)} %copy-done, bf16[1024,256]{1,0:T(8,128)(2,1)S(1)} %collective-permute-done.1.other_ref), custom_call_target="tpu_custom_call" | custom-call | tf_op jit(solution)/shard_map/project/pallas_call | solution.py:301
  79.6 14.6 %all_to_all.20.x_ref = bf16[16,16,256]{2,1,0:T(8,128)(2,1)S(1)} all-to-all(bf16[16,16,256]{2,1,0:T(8,128)(2,1)S(1)} %project.1), channel_id=1, replica_groups=mesh['zh'=4,'zl'=2,'yh'=4,'yl'=2,'head'=8] {'zl','head'}, dimensions={0} | all-to-all | bytes 262144 | tf_op jit(solution)/shard_map/all_to_all | solution.py:241
  94.1 0.6 sum.1
  (2 shorter events, 0.1 us)
Async XLA Ops:
  0.0 0.7 copy-start.5
  1.4 16.7 %copy-start.1 = (bf16[512,128]{1,0:T(8,128)(2,1)S(1)}, bf16[512,128]{1,0:T(8,128)(2,1)}, u32[]{:S(2)}) copy-start(bf16[512,128]{1,0:T(8,128)(2,1)} %k_ref.1) | copy-start | bytes 393220
  1.4 16.7 %copy-start.2 = (bf16[512,128]{1,0:T(8,128)(2,1)S(1)}, bf16[512,128]{1,0:T(8,128)(2,1)}, u32[]{:S(2)}) copy-start(bf16[512,128]{1,0:T(8,128)(2,1)} %v_ref.1) | copy-start | bytes 393220
  1.4 16.7 %copy-start.7 = (s32[64,1,8]{0,2,1:T(8,128)S(1)}, s32[64,1,8]{0,2,1:T(8,128)}, u32[]{:S(2)}) copy-start(s32[64,1,8]{0,2,1:T(8,128)} %param.13) | copy-start | bytes 6148
  1.4 29.3 %all-to-all-start = ((bf16[32,32,128]{2,1,0:T(8,128)(2,1)}), bf16[32,32,128]{2,1,0:T(8,128)(2,1)S(1)}, u32[]{:S(2)}, u32[]{:S(2)}) async-start(bf16[32,32,128]{2,1,0:T(8,128)(2,1)} %spread.1), calls=%async_computation | async-start | bytes 524288 | tf_op jit(solution)/shard_map/all_to_all | solution.py:241
  18.1 3.2 %copy-start.3 = (bf16[1,256,128]{2,1,0:T(8,128)(2,1)S(1)}, bf16[1,256,128]{2,1,0:T(8,128)(2,1)}, u32[]{:S(2)}) copy-start(bf16[1,256,128]{2,1,0:T(8,128)(2,1)} %param.14) | copy-start | bytes 196612
  18.1 3.2 %copy-start.4 = (bf16[1,256,128]{2,1,0:T(8,128)(2,1)S(1)}, bf16[1,256,128]{2,1,0:T(8,128)(2,1)}, u32[]{:S(2)}) copy-start(bf16[1,256,128]{2,1,0:T(8,128)(2,1)} %param.15) | copy-start | bytes 196612
  18.2 3.2 %copy-start.6 = (bf16[2,1,2048]{2,0,1:T(2,128)(2,1)S(1)}, bf16[2,1,2048]{2,0,1:T(2,128)(2,1)}, u32[]{:S(2)}) copy-start(bf16[2,1,2048]{2,0,1:T(2,128)(2,1)} %param.10) | copy-start | bytes 24580
  18.2 3.2 %copy-start.8 = (bf16[2,1,128]{2,0,1:T(2,128)(2,1)S(1)}, bf16[2,1,128]{2,0,1:T(2,128)(2,1)}, u32[]{:S(2)}) copy-start(bf16[2,1,128]{2,0,1:T(2,128)(2,1)} %param.16) | copy-start | bytes 1540
  18.2 3.2 %copy-start.9 = (bf16[2,1,128]{2,0,1:T(2,128)(2,1)S(1)}, bf16[2,1,128]{2,0,1:T(2,128)(2,1)}, u32[]{:S(2)}) copy-start(bf16[2,1,128]{2,0,1:T(2,128)(2,1)} %param.17) | copy-start | bytes 1540
  18.2 27.1 %copy-start = (bf16[2048,256]{1,0:T(8,128)(2,1)S(1)}, bf16[2048,256]{1,0:T(8,128)(2,1)}, u32[]{:S(2)}) copy-start(bf16[2048,256]{1,0:T(8,128)(2,1)} %w_ref.1) | copy-start | bytes 3145732
  18.2 12.5 %collective-permute-start = (bf16[1040,128]{1,0:T(8,128)(2,1)S(1)}, bf16[1040,128]{1,0:T(8,128)(2,1)S(1)}, u32[]{:S(2)}, u32[]{:S(2)}) collective-permute-start(bf16[1040,128]{1,0:T(8,128)(2,1)S(1)} %pack.1.here_ref), channel_id=1, source_target_pairs={{0,8},{8,0},{1,9},{9,1},{2,10},{10,2},{3,11},{11,3},{4,12},{12,4},... | collective-permute-start | bytes 798728 | tf_op jit(solution)/shard_map/ppermute | solution.py:274
  34.1 24.7 %all-to-all-start.1 = ((bf16[32,40,128]{2,1,0:T(8,128)(2,1)}), bf16[32,40,128]{2,1,0:T(8,128)(2,1)S(1)}, u32[]{:S(2)}, u32[]{:S(2)}) async-start(bf16[32,40,128]{2,1,0:T(8,128)(2,1)} %prompt.1), calls=%async_computation.1 | async-start | bytes 655360 | tf_op jit(solution)/shard_map/all_to_all | solution.py:241
  45.4 21.1 %collective-permute-start.1 = (bf16[1024,256]{1,0:T(8,128)(2,1)S(1)}, bf16[1024,256]{1,0:T(8,128)(2,1)S(1)}, u32[]{:S(2)}, u32[]{:S(2)}) collective-permute-start(bf16[1024,256]{1,0:T(8,128)(2,1)S(1)} %constant_dynamic-slice_fusion), channel_id=1, source_target_pairs={{0,64},{64,0},{1,65},{65,1},{2,66},{66,2},{3,67},{67,3},{4,68},{68... | collective-permute-start | bytes 1572872 | tf_op jit(solution)/shard_map/ppermute | solution.py:275
  59.7 18.8 %all-to-all-start.2 = ((bf16[32,32,128]{2,1,0:T(8,128)(2,1)}), bf16[32,32,128]{2,1,0:T(8,128)(2,1)S(1)}, u32[]{:S(2)}, u32[]{:S(2)}) async-start(bf16[32,32,128]{2,1,0:T(8,128)(2,1)} %combine.1), calls=%async_computation.2 | async-start | bytes 524288 | tf_op jit(solution)/shard_map/all_to_all | solution.py:241

commit v3 on v1

--- a/solution.py
+++ b/solution.py
@@ -5,6 +5,7 @@
 from jax import lax
 from jax.experimental import pallas as pl
 from jax.experimental.pallas import tpu as pltpu
+from jax.sharding import Mesh
 from jax.sharding import PartitionSpec as P
 
 HD = 128
@@ -13,9 +14,13 @@
 STEPS = 2
 ITEM = STEPS * PER
 STAT = 8
+FLAG = 16
 NEGATIVE = -1e30
 SCALE = math.log2(math.e) / math.sqrt(HD)
-TILE = 8
+TILE = 4
+CTX = ("zh", "zl", "yh", "yl")
+FAR = ("zh", "yh")
+NEAR = ("zl", "yl")
 
 VMEM = pl.BlockSpec(memory_space=pltpu.VMEM)
 SMEM = pl.BlockSpec(memory_space=pltpu.SMEM)
@@ -56,9 +61,20 @@
     out_ref[...] = jnp.broadcast_to(rows[None], out_ref.shape)
 
 
-def own_kernel(
-    q_ref, sel_ref, ck_ref, cv_ref, nk_ref, nv_ref, pos_ref, bias_ref, out_ref, log_ref, rows_ref
-):
+def pack_kernel(k_ref, v_ref, sel_ref, out_ref):
+    tokens = k_ref.shape[0]
+    out_ref[:tokens, :] = k_ref[...]
+    out_ref[tokens : 2 * tokens, :] = v_ref[...]
+    slots, samples = sel_ref.shape
+    number = iota((FLAG, samples), 0)
+    bias = jnp.full((FLAG, samples), NEGATIVE, F32)
+    for slot in range(slots):
+        bias = jnp.where(sel_ref[slot : slot + 1, :] == number, 0.0, bias)
+    bias = jnp.concatenate([bias, jnp.zeros((FLAG, HD - samples), F32)], axis=1)
+    out_ref[2 * tokens :, :] = bias.astype(BF16)
+
+
+def own_kernel(q_ref, ck_ref, cv_ref, nk_ref, nv_ref, pos_ref, out_ref, log_ref, rows_ref):
     rows = item_rows(q_ref, rows_ref)
     slots = ck_ref.shape[0]
     scores = dot_t(rows.astype(BF16), ck_ref[...]) * SCALE
@@ -84,35 +100,39 @@
     out_ref[...] = total / mass
     log_mass = jnp.broadcast_to(top + jnp.log2(mass), (ITEM, HD))
     log_ref[...] = jnp.broadcast_to(to_lanes(log_mass, 1), log_ref.shape)
-    slot_count, samples = sel_ref.shape
-    tokens = bias_ref.shape[1]
-    blocks = tokens // BLOCK
-    number = iota((blocks, samples), 0)
-    chosen = jnp.zeros((blocks, samples), F32)
-    for slot in range(slot_count):
-        chosen = jnp.where(sel_ref[slot : slot + 1, :] == number, 1.0, chosen)
-    widen = (iota((blocks, tokens), 1) // BLOCK == iota((blocks, tokens), 0)).astype(F32)
-    hit = lax.dot_general(chosen, widen, (((0,), (0,)), ((), ())), preferred_element_type=F32)
-    bias_ref[...] = jnp.where(hit > 0.5, 0.0, NEGATIVE)
-
-
-def prompt_kernel(q_ref, k_ref, v_ref, bias_ref, out_ref):
+
+
+def prompt_kernel(place_ref, q_ref, *refs):
+    *pack_refs, out_ref, keys_ref = refs
     samples = q_ref.shape[0]
-    tokens = k_ref.shape[0]
-    keys = k_ref[...]
-    values = jnp.concatenate([v_ref[...], jnp.ones((tokens, HD), BF16)], axis=1)
+    tokens = (pack_refs[0].shape[0] - FLAG) // 2
+    widen = iota((tokens, FLAG), 0) // BLOCK == iota((tokens, FLAG), 1)
+    widen = widen.astype(F32).astype(BF16)
+    for index, ref in enumerate(pack_refs):
+        keys_ref[index, :, :HD] = ref[:tokens, :]
+        keys_ref[index, :, HD:] = dot(widen, ref[2 * tokens :, :]).astype(BF16)
+    ones = jnp.ones((tokens, HD), BF16)
+    count = TILE * ITEM
+    number = iota((count, HD), 0) // ITEM
     for first in range(0, samples, TILE):
         here = slice(first, first + TILE)
-        q = q_ref[here].reshape(TILE * ITEM, HD)
-        scores = dot_t(q, keys) * SCALE
-        scores = scores.reshape(TILE, ITEM, tokens) + bias_ref[here][:, None, :]
-        scores = scores.reshape(TILE * ITEM, tokens)
-        top = jnp.max(scores, axis=1, keepdims=True)
-        weights = jnp.exp2(scores - top).astype(BF16)
-        total = dot(weights, values)
+        q = q_ref[here].reshape(count, HD)
+        sample = (first + number) // 4 * 16 + (first + number) % 4 * 2 + place_ref[0]
+        mine = (iota((count, HD), 1) == sample).astype(F32).astype(BF16)
+        q = jnp.concatenate([q, mine], axis=1)
+        scores = [dot_t(q, keys_ref[index]) for index in range(len(pack_refs))]
+        top = scores[0]
+        for score in scores[1:]:
+            top = jnp.maximum(top, score)
+        top = jnp.max(top, axis=1, keepdims=True)
+        total = jnp.zeros((count, 2 * HD), F32)
+        for score, ref in zip(scores, pack_refs):
+            weights = jnp.exp2((score - top) * SCALE).astype(BF16)
+            values = jnp.concatenate([ref[tokens : 2 * tokens, :], ones], axis=1)
+            total = total + dot(weights, values)
         mass = total[:, HD:]
         out_ref[here, :ITEM, :] = (total[:, :HD] / mass).astype(BF16).reshape(TILE, ITEM, HD)
-        log_mass = to_lanes(top + jnp.log2(mass), TILE)
+        log_mass = to_lanes(top * SCALE + jnp.log2(mass), TILE)
         high = log_mass.astype(BF16).astype(F32)
         rest = log_mass - high
         middle = rest.astype(BF16).astype(F32)
@@ -200,8 +220,8 @@
     )
 
 
-def swap(array, axis):
-    return lax.all_to_all(array, axis, split_axis=0, concat_axis=0, tiled=True)
+def swap(array, axes):
+    return lax.all_to_all(array, axes, split_axis=0, concat_axis=0, tiled=True)
 
 
 def shards(
@@ -216,74 +236,80 @@
     positions,
     out_weight,
 ):
-    samples = lax.axis_size("ctx")
-    parts = lax.axis_size("head")
+    struct = jax.ShapeDtypeStruct
+    samples = lax.axis_size(CTX)
+    far = lax.axis_size(FAR)
+    heads = lax.axis_size("head")
     tokens = prompt_keys.shape[0]
     columns = out_weight.shape[1]
-    struct = jax.ShapeDtypeStruct
+    place = (8 * lax.axis_index("zl") + lax.axis_index("yl")).astype(jnp.int32).reshape(1)
     rows_scratch = pltpu.VMEM((ITEM, HD), F32)
     q = queries.reshape(STEPS, PER * HD)
+
     spread = call(
-        spread_kernel, "spread", struct((samples, ITEM, HD), BF16), [VMEM], VMEM, [rows_scratch]
+        spread_kernel, "spread", struct((far, ITEM, HD), BF16), [VMEM], VMEM, [rows_scratch]
     )(q)
-    gathered = swap(spread, "ctx")
-    bias, own, own_log = call(
+    here = call(
+        pack_kernel, "pack", struct((2 * tokens + FLAG, HD), BF16), [VMEM] * 3, VMEM
+    )(prompt_keys, prompt_values, selected[:, 0, :].T)
+    gathered = swap(spread, FAR)
+    packs = [
+        here,
+        lax.ppermute(here, "yl", [(0, 1), (1, 0)]),
+        lax.ppermute(here, "zl", [(0, 1), (1, 0)]),
+        lax.ppermute(here, NEAR, [(0, 3), (1, 2), (2, 1), (3, 0)]),
+    ]
+    own, own_log = call(
         own_kernel,
         "own",
-        (struct((samples, tokens), F32), struct((ITEM, HD), F32), struct((8, HD), F32)),
-        [VMEM] * 6 + [SMEM],
-        (VMEM, VMEM, VMEM),
+        (struct((ITEM, HD), F32), struct((8, HD), F32)),
+        [VMEM] * 5 + [SMEM],
+        (VMEM, VMEM),
         [rows_scratch],
         flops=10**6,
         moved=3 * 10**5,
-    )(
-        q,
-        selected[:, 0, :].T,
-        cache_keys[0],
-        cache_values[0],
-        new_keys[:, 0],
-        new_values[:, 0],
-        positions,
-    )
-    parts_out = call(
+    )(q, cache_keys[0], cache_values[0], new_keys[:, 0], new_values[:, 0], positions)
+    partial = call(
         prompt_kernel,
         "prompt",
-        struct((samples, ITEM + STAT, HD), BF16),
-        [VMEM] * 4,
+        struct((far, ITEM + STAT, HD), BF16),
+        [SMEM] + [VMEM] * 5,
         VMEM,
-    )(gathered, prompt_keys, prompt_values, bias)
-    received = swap(parts_out, "ctx")
+        [pltpu.VMEM((4, tokens, 2 * HD), BF16)],
+    )(place, gathered, *packs)
+    received = swap(partial, FAR)
     attended = call(
         combine_kernel, "combine", struct((samples, ITEM, HD), BF16), [VMEM] * 3, VMEM
     )(received, own, own_log)
-    every = swap(attended, "ctx")
+    every = swap(attended, CTX)
     product = call(
         project_kernel,
         "project",
-        struct((parts, STEPS * samples // parts, columns), F32),
+        struct((heads, STEPS * samples // heads, columns), F32),
         [VMEM] * 2,
         VMEM,
         [pltpu.VMEM((samples * ITEM, HD), F32)],
     )(every, out_weight)
     terms = swap(product, "head")
     return call(
-        sum_kernel, "sum", struct((STEPS, samples // parts, columns), BF16), [VMEM], VMEM
+        sum_kernel, "sum", struct((STEPS, samples // heads, columns), BF16), [VMEM], VMEM
     )(terms)
 
 
 def solution(mesh):
+    fine = Mesh(mesh.devices.reshape(4, 2, 4, 2, 8), (*CTX, "head"))
     placed = (
-        P(None, "ctx", "head"),
-        P("ctx", "head"),
-        P("ctx", "head"),
-        P(None, "head", "ctx"),
-        P("ctx", None, "head"),
-        P("ctx", None, "head"),
-        P(None, "ctx", "head"),
-        P(None, "ctx", "head"),
-        P("ctx"),
-        P("head", "ctx"),
+        P(None, CTX, "head"),
+        P(CTX, "head"),
+        P(CTX, "head"),
+        P(None, "head", CTX),
+        P(CTX, None, "head"),
+        P(CTX, None, "head"),
+        P(None, CTX, "head"),
+        P(None, CTX, "head"),
+        P(CTX),
+        P("head", CTX),
     )
     return jax.shard_map(
-        shards, mesh=mesh, in_specs=placed, out_specs=P(None, "head", "ctx"), check_vma=False
+        shards, mesh=fine, in_specs=placed, out_specs=P(None, "head", CTX), check_vma=False
     )

time: 102 us -> 95.1 us (0.932)
  blocking collectives: 62.7 us -> 34.9 us
  starting transfers between devices: 17.3 us -> 28.2 us
  waiting for transfers between devices: 16 us -> 21.8 us
  local copies, waits for them, and re-layouts: 0.74 us -> 2.53 us
  Pallas kernels: 4.63 us -> 6.4 us
    all_to_all x3 -> x2, blocking collectives: 62.7 us -> 34.9 us  [swap(): return lax.all_to_all(array, axes, split_axis=0, concat_axis=0, tiled=True)]
    ppermute x0 -> x3, starting transfers between devices: none -> 9.96 us  [the longest x1 4.03 us: shards(): lax.ppermute(here, 'yl', [(0, 1), (1, 0)])]
    all_to_all x1 -> x2, waiting for transfers between devices: 16 us -> 21.8 us  [swap(): return lax.all_to_all(array, axes, split_axis=0, concat_axis=0, tiled=True)]
    pallas_call x5 -> x6, Pallas kernels: 4.27 us -> 6.17 us  [the longest x1 3.7 us: shards(): call(prompt_kernel, 'prompt', struct((far, ITEM + STAT, HD), BF16), [SMEM...]
    unnamed x20 -> x18, local copies, waits for them, and re-layouts: 0.74 us -> 2.53 us
    all_to_all x1 -> x2, starting transfers between devices: 17.3 us -> 18.3 us  [swap(): return lax.all_to_all(array, axes, split_axis=0, concat_axis=0, tiled=True)]
  transfers between devices with their start and end apart: 1 -> 5, of which waited for: 1 -> 2; matrix products, arithmetic and copies ran while one was open for 0% -> 0% of each run, Pallas kernels for 0% -> 1%
where the time goes in v3:
time: 95.1 us; the launch traced here: 94.6 us
  blocking collectives  34.9 us (37%)
  starting transfers between devices  28.2 us (30%)
  waiting for transfers between devices  21.8 us (23%)
  Pallas kernels  6.4 us (7%)
  local copies, waits for them, and re-layouts  2.53 us (3%)
    all_to_all x2, blocking collectives, swap(): return lax.all_to_all(array, axes, split_axis=0, concat_axis=0, tiled=True)  34.9 us
    all_to_all x2, waiting for transfers between devices, swap(): return lax.all_to_all(array, axes, split_axis=0, concat_axis=0, tiled=True)  21.8 us
    all_to_all x2, starting transfers between devices, swap(): return lax.all_to_all(array, axes, split_axis=0, concat_axis=0, tiled=True)  18.3 us
    ppermute x1, starting transfers between devices, shards(): lax.ppermute(here, 'yl', [(0, 1), (1, 0)])  4.03 us
    ppermute x1, starting transfers between devices, shards(): lax.ppermute(here, 'zl', [(0, 1), (1, 0)])  4 us
    pallas_call x1, Pallas kernels, shards(): call(prompt_kernel, 'prompt', struct((far, ITEM + STAT, HD), BF16), [SMEM...  3.7 us
    unnamed x18, local copies, waits for them, and re-layouts  2.53 us
    ppermute x1, starting transfers between devices, shards(): lax.ppermute(here, NEAR, [(0, 3), (1, 2), (2, 1), (3, 0)])  1.92 us
  transfers between devices with their start and end apart: 5, of which 2 were waited for; matrix products, arithmetic and copies ran while one was open for 0% of the time, Pallas kernels for 1%

profile of v3, /device:TPU:1, one launch (start us, length us, event | category | flops | bytes accessed | tf_op | source)
XLA Modules:
  0.0 94.6 jit_solution(12452432308844823631)
XLA Ops:
  0.0 0.0 copy-start.1
  0.0 0.9 copy-done.1
  0.9 0.0 copy-start.2
  0.9 0.9 copy-done.2
  1.8 0.0 copy-start.6
  1.8 0.7 copy-done.6
  2.5 0.0 copy-start.5
  2.5 4.0 %collective-permute-start = (bf16[1040,128]{1,0:T(8,128)(2,1)S(1)}, bf16[1040,128]{1,0:T(8,128)(2,1)S(1)}, u32[]{:S(2)}, u32[]{:S(2)}) collective-permute-start(bf16[1040,128]{1,0:T(8,128)(2,1)S(1)} %pack.1.refs_0_), channel_id=1, source_target_pairs={{0,8},{8,0},{1,9},{9,1},{2,10},{10,2},{3,11},{11,3},{4,12},{12,4},... | collective-permute-start | bytes 798728 | tf_op jit(solution)/shard_map/ppermute | solution.py:258
  6.6 4.0 %collective-permute-start.1 = (bf16[1040,128]{1,0:T(8,128)(2,1)S(1)}, bf16[1040,128]{1,0:T(8,128)(2,1)S(1)}, u32[]{:S(2)}, u32[]{:S(2)}) collective-permute-start(bf16[1040,128]{1,0:T(8,128)(2,1)S(1)} %pack.1.refs_0_), channel_id=1, source_target_pairs={{0,64},{64,0},{1,65},{65,1},{2,66},{66,2},{3,67},{67,3},{4,68},{68... | collective-permute-start | bytes 798728 | tf_op jit(solution)/shard_map/ppermute | solution.py:259
  10.6 1.9 %collective-permute-start.2 = (bf16[1040,128]{1,0:T(8,128)(2,1)S(1)}, bf16[1040,128]{1,0:T(8,128)(2,1)S(1)}, u32[]{:S(2)}, u32[]{:S(2)}) collective-permute-start(bf16[1040,128]{1,0:T(8,128)(2,1)S(1)} %pack.1.refs_0_), channel_id=1, source_target_pairs={{0,72},{8,64},{64,8},{72,0},{1,73},{9,65},{65,9},{73,1},{2,74},{10... | collective-permute-start | bytes 798728 | tf_op jit(solution)/shard_map/ppermute | solution.py:260
  12.5 0.0 copy-done.5
  12.5 0.7 spread.1
  13.2 14.6 %all-to-all-start = ((bf16[16,32,128]{2,1,0:T(8,128)(2,1)}), bf16[16,32,128]{2,1,0:T(8,128)(2,1)S(1)}, u32[]{:S(2)}, u32[]{:S(2)}) async-start(bf16[16,32,128]{2,1,0:T(8,128)(2,1)} %spread.1), calls=%async_computation | async-start | bytes 262144 | tf_op jit(solution)/shard_map/all_to_all | solution.py:224
  27.9 11.4 %all-to-all-done.q_ref = bf16[16,32,128]{2,1,0:T(8,128)(2,1)S(1)} async-done(((bf16[16,32,128]{2,1,0:T(8,128)(2,1)}), bf16[16,32,128]{2,1,0:T(8,128)(2,1)S(1)}, u32[]{:S(2)}, u32[]{:S(2)}) %all-to-all-start) | async-done | bytes 131104 | tf_op jit(solution)/shard_map/all_to_all | solution.py:224
  39.3 0.0 collective-permute-done.refs_1_
  39.3 0.0 collective-permute-done.1.refs_2_
  39.3 0.0 collective-permute-done.2.refs_3_
  39.3 0.0 copy-start.3
  39.3 0.0 copy-start.4
  39.3 0.0 copy-start.7
  39.3 0.0 copy-start.8
  39.3 3.7 %prompt.1 = bf16[16,40,128]{2,1,0:T(8,128)(2,1)} custom-call(s32[1]{0:T(128)} %bitcast.place_ref, bf16[16,32,128]{2,1,0:T(8,128)(2,1)S(1)} %all-to-all-done.q_ref, bf16[1040,128]{1,0:T(8,128)(2,1)S(1)} %pack.1.refs_0_, bf16[1040,128]{1,0:T(8,128)(2,1)S(1)} %collective-permute-done.refs_1_, bf16[1040,128]{1,0:T(8,128)(2,1)S(1)} %collective-permute-done.1.refs_2_, ...), custom_call_target="tpu_custom_call" | custom-call | tf_op jit(solution)/shard_map/prompt/pallas_call | solution.py:272
  43.0 0.0 copy-start
  43.0 3.6 %all-to-all-start.1 = ((bf16[16,40,128]{2,1,0:T(8,128)(2,1)}), bf16[16,40,128]{2,1,0:T(8,128)(2,1)S(1)}, u32[]{:S(2)}, u32[]{:S(2)}) async-start(bf16[16,40,128]{2,1,0:T(8,128)(2,1)} %prompt.1), calls=%async_computation.1 | async-start | bytes 327680 | tf_op jit(solution)/shard_map/all_to_all | solution.py:224
  47.3 0.0 copy-done.3
  47.3 0.0 copy-done.4
  47.4 0.0 copy-done.7
  47.4 0.0 copy-done.8
  47.4 0.4 own.1
  47.7 10.3 %all-to-all-done.1.part_ref = bf16[16,40,128]{2,1,0:T(8,128)(2,1)S(1)} async-done(((bf16[16,40,128]{2,1,0:T(8,128)(2,1)}), bf16[16,40,128]{2,1,0:T(8,128)(2,1)S(1)}, u32[]{:S(2)}, u32[]{:S(2)}) %all-to-all-start.1) | async-done | bytes 163872 | tf_op jit(solution)/shard_map/all_to_all | solution.py:224
  58.1 0.2 combine.1
  58.3 19.7 %all_to_all.20.x_ref = bf16[64,32,128]{2,1,0:T(8,128)(2,1)S(1)} all-to-all(bf16[64,32,128]{2,1,0:T(8,128)(2,1)S(1)} %combine.1), channel_id=1, replica_groups=mesh['zh'=4,'zl'=2,'yh'=4,'yl'=2,'head'=8] {'zh','zl','yh','yl'}, dimensions={0} | all-to-all | bytes 1048576 | tf_op jit(solution)/shard_map/all_to_all | solution.py:224
  78.0 0.0 copy-done
  78.0 0.8 project.1
  78.8 15.2 %all_to_all.21.x_ref = f32[8,16,256]{2,1,0:T(8,128)S(1)} all-to-all(f32[8,16,256]{2,1,0:T(8,128)S(1)} %project.1), channel_id=1, replica_groups=mesh['zh'=4,'zl'=2,'yh'=4,'yl'=2,'head'=8] {'head'}, dimensions={0} | all-to-all | bytes 262144 | tf_op jit(solution)/shard_map/all_to_all | solution.py:224
  94.0 0.6 sum.1
  (1 shorter events, 0.0 us)
Async XLA Ops:
  0.0 0.9 copy-start.1
  0.9 0.9 copy-start.2
  1.8 0.7 copy-start.6
  2.5 10.0 %copy-start.5 = (bf16[2,1,2048]{2,0,1:T(2,128)(2,1)S(1)}, bf16[2,1,2048]{2,0,1:T(2,128)(2,1)}, u32[]{:S(2)}) copy-start(bf16[2,1,2048]{2,0,1:T(2,128)(2,1)} %param.10) | copy-start | bytes 24580
  2.5 36.7 %collective-permute-start = (bf16[1040,128]{1,0:T(8,128)(2,1)S(1)}, bf16[1040,128]{1,0:T(8,128)(2,1)S(1)}, u32[]{:S(2)}, u32[]{:S(2)}) collective-permute-start(bf16[1040,128]{1,0:T(8,128)(2,1)S(1)} %pack.1.refs_0_), channel_id=1, source_target_pairs={{0,8},{8,0},{1,9},{9,1},{2,10},{10,2},{3,11},{11,3},{4,12},{12,4},... | collective-permute-start | bytes 798728 | tf_op jit(solution)/shard_map/ppermute | solution.py:258
  6.6 32.7 %collective-permute-start.1 = (bf16[1040,128]{1,0:T(8,128)(2,1)S(1)}, bf16[1040,128]{1,0:T(8,128)(2,1)S(1)}, u32[]{:S(2)}, u32[]{:S(2)}) collective-permute-start(bf16[1040,128]{1,0:T(8,128)(2,1)S(1)} %pack.1.refs_0_), channel_id=1, source_target_pairs={{0,64},{64,0},{1,65},{65,1},{2,66},{66,2},{3,67},{67,3},{4,68},{68... | collective-permute-start | bytes 798728 | tf_op jit(solution)/shard_map/ppermute | solution.py:259
  10.6 28.7 %collective-permute-start.2 = (bf16[1040,128]{1,0:T(8,128)(2,1)S(1)}, bf16[1040,128]{1,0:T(8,128)(2,1)S(1)}, u32[]{:S(2)}, u32[]{:S(2)}) collective-permute-start(bf16[1040,128]{1,0:T(8,128)(2,1)S(1)} %pack.1.refs_0_), channel_id=1, source_target_pairs={{0,72},{8,64},{64,8},{72,0},{1,73},{9,65},{65,9},{73,1},{2,74},{10... | collective-permute-start | bytes 798728 | tf_op jit(solution)/shard_map/ppermute | solution.py:260
  13.2 26.1 %all-to-all-start = ((bf16[16,32,128]{2,1,0:T(8,128)(2,1)}), bf16[16,32,128]{2,1,0:T(8,128)(2,1)S(1)}, u32[]{:S(2)}, u32[]{:S(2)}) async-start(bf16[16,32,128]{2,1,0:T(8,128)(2,1)} %spread.1), calls=%async_computation | async-start | bytes 262144 | tf_op jit(solution)/shard_map/all_to_all | solution.py:224
  39.3 8.1 %copy-start.3 = (bf16[1,256,128]{2,1,0:T(8,128)(2,1)S(1)}, bf16[1,256,128]{2,1,0:T(8,128)(2,1)}, u32[]{:S(2)}) copy-start(bf16[1,256,128]{2,1,0:T(8,128)(2,1)} %param.14) | copy-start | bytes 196612
  39.3 8.1 %copy-start.4 = (bf16[1,256,128]{2,1,0:T(8,128)(2,1)S(1)}, bf16[1,256,128]{2,1,0:T(8,128)(2,1)}, u32[]{:S(2)}) copy-start(bf16[1,256,128]{2,1,0:T(8,128)(2,1)} %param.15) | copy-start | bytes 196612
  39.3 8.1 %copy-start.7 = (bf16[2,1,128]{2,0,1:T(2,128)(2,1)S(1)}, bf16[2,1,128]{2,0,1:T(2,128)(2,1)}, u32[]{:S(2)}) copy-start(bf16[2,1,128]{2,0,1:T(2,128)(2,1)} %param.16) | copy-start | bytes 1540
  39.3 8.1 %copy-start.8 = (bf16[2,1,128]{2,0,1:T(2,128)(2,1)S(1)}, bf16[2,1,128]{2,0,1:T(2,128)(2,1)}, u32[]{:S(2)}) copy-start(bf16[2,1,128]{2,0,1:T(2,128)(2,1)} %param.17) | copy-start | bytes 1540
  43.0 35.0 %copy-start = (bf16[2048,256]{1,0:T(8,128)(2,1)S(1)}, bf16[2048,256]{1,0:T(8,128)(2,1)}, u32[]{:S(2)}) copy-start(bf16[2048,256]{1,0:T(8,128)(2,1)} %w_ref.1) | copy-start | bytes 3145732
  43.0 15.0 %all-to-all-start.1 = ((bf16[16,40,128]{2,1,0:T(8,128)(2,1)}), bf16[16,40,128]{2,1,0:T(8,128)(2,1)S(1)}, u32[]{:S(2)}, u32[]{:S(2)}) async-start(bf16[16,40,128]{2,1,0:T(8,128)(2,1)} %prompt.1), calls=%async_computation.1 | async-start | bytes 327680 | tf_op jit(solution)/shard_map/all_to_all | solution.py:224

commit v4 on v3

--- a/solution.py
+++ b/solution.py
@@ -18,9 +18,9 @@
 NEGATIVE = -1e30
 SCALE = math.log2(math.e) / math.sqrt(HD)
 TILE = 4
-CTX = ("zh", "zl", "yh", "yl")
-FAR = ("zh", "yh")
-NEAR = ("zl", "yl")
+CTX = ("z", "yh", "yl")
+FAR = ("z", "yh")
+NEAR = "yl"
 
 VMEM = pl.BlockSpec(memory_space=pltpu.VMEM)
 SMEM = pl.BlockSpec(memory_space=pltpu.SMEM)
@@ -106,21 +106,26 @@
     *pack_refs, out_ref, keys_ref = refs
     samples = q_ref.shape[0]
     tokens = (pack_refs[0].shape[0] - FLAG) // 2
-    widen = iota((tokens, FLAG), 0) // BLOCK == iota((tokens, FLAG), 1)
+    widen = iota((FLAG, tokens), 1) // BLOCK == iota((FLAG, tokens), 0)
     widen = widen.astype(F32).astype(BF16)
     for index, ref in enumerate(pack_refs):
-        keys_ref[index, :, :HD] = ref[:tokens, :]
-        keys_ref[index, :, HD:] = dot(widen, ref[2 * tokens :, :]).astype(BF16)
+        place = slice(index * tokens, (index + 1) * tokens)
+        keys_ref[:HD, place] = ref[:tokens, :].T
+        bias = lax.dot_general(
+            ref[2 * tokens :, :], widen, (((0,), (0,)), ((), ())), preferred_element_type=F32
+        )
+        keys_ref[HD:, place] = bias.astype(BF16)
     ones = jnp.ones((tokens, HD), BF16)
     count = TILE * ITEM
     number = iota((count, HD), 0) // ITEM
     for first in range(0, samples, TILE):
         here = slice(first, first + TILE)
         q = q_ref[here].reshape(count, HD)
-        sample = (first + number) // 4 * 16 + (first + number) % 4 * 2 + place_ref[0]
-        mine = (iota((count, HD), 1) == sample).astype(F32).astype(BF16)
-        q = jnp.concatenate([q, mine], axis=1)
-        scores = [dot_t(q, keys_ref[index]) for index in range(len(pack_refs))]
+        mine = iota((count, HD), 1) == 2 * (first + number) + place_ref[0]
+        q = jnp.concatenate([q, mine.astype(F32).astype(BF16)], axis=1)
+        scores = []
+        for index in range(len(pack_refs)):
+            scores.append(dot(q, keys_ref[:, index * tokens : (index + 1) * tokens]))
         top = scores[0]
         for score in scores[1:]:
             top = jnp.maximum(top, score)
@@ -242,7 +247,7 @@
     heads = lax.axis_size("head")
     tokens = prompt_keys.shape[0]
     columns = out_weight.shape[1]
-    place = (8 * lax.axis_index("zl") + lax.axis_index("yl")).astype(jnp.int32).reshape(1)
+    place = lax.axis_index(NEAR).astype(jnp.int32).reshape(1)
     rows_scratch = pltpu.VMEM((ITEM, HD), F32)
     q = queries.reshape(STEPS, PER * HD)
 
@@ -253,12 +258,7 @@
         pack_kernel, "pack", struct((2 * tokens + FLAG, HD), BF16), [VMEM] * 3, VMEM
     )(prompt_keys, prompt_values, selected[:, 0, :].T)
     gathered = swap(spread, FAR)
-    packs = [
-        here,
-        lax.ppermute(here, "yl", [(0, 1), (1, 0)]),
-        lax.ppermute(here, "zl", [(0, 1), (1, 0)]),
-        lax.ppermute(here, NEAR, [(0, 3), (1, 2), (2, 1), (3, 0)]),
-    ]
+    there = lax.ppermute(here, NEAR, [(0, 1), (1, 0)])
     own, own_log = call(
         own_kernel,
         "own",
@@ -273,10 +273,10 @@
         prompt_kernel,
         "prompt",
         struct((far, ITEM + STAT, HD), BF16),
-        [SMEM] + [VMEM] * 5,
+        [SMEM] + [VMEM] * 3,
         VMEM,
-        [pltpu.VMEM((4, tokens, 2 * HD), BF16)],
-    )(place, gathered, *packs)
+        [pltpu.VMEM((2 * HD, 2 * tokens), BF16)],
+    )(place, gathered, here, there)
     received = swap(partial, FAR)
     attended = call(
         combine_kernel, "combine", struct((samples, ITEM, HD), BF16), [VMEM] * 3, VMEM
@@ -297,7 +297,7 @@
 
 
 def solution(mesh):
-    fine = Mesh(mesh.devices.reshape(4, 2, 4, 2, 8), (*CTX, "head"))
+    fine = Mesh(mesh.devices.reshape(8, 4, 2, 8), (*CTX, "head"))
     placed = (
         P(None, CTX, "head"),
         P(CTX, "head"),

time: 95.1 us -> 96.9 us (1.019)
  starting transfers between devices: 28.2 us -> 30.3 us
  blocking collectives: 34.9 us -> 36.9 us
  local copies, waits for them, and re-layouts: 2.53 us -> 0.73 us
  Pallas kernels: 6.4 us -> 5.37 us
    ppermute x3 -> x1, waiting for transfers between devices: 0.01 us -> 10.1 us  [shards(): there = lax.ppermute(here, NEAR, [(0, 1), (1, 0)])]
    all_to_all x2, starting transfers between devices: 18.3 us -> 28 us  [swap(): return lax.all_to_all(array, axes, split_axis=0, concat_axis=0, tiled=True)]
    all_to_all x2, waiting for transfers between devices: 21.8 us -> 12.1 us  [swap(): return lax.all_to_all(array, axes, split_axis=0, concat_axis=0, tiled=True)]
    ppermute x3 -> x1, starting transfers between devices: 9.96 us -> 2.31 us  [shards(): there = lax.ppermute(here, NEAR, [(0, 1), (1, 0)])]
    all_to_all x2, blocking collectives: 34.9 us -> 36.9 us  [swap(): return lax.all_to_all(array, axes, split_axis=0, concat_axis=0, tiled=True)]
    unnamed x18 -> x20, local copies, waits for them, and re-layouts: 2.53 us -> 0.73 us
    pallas_call x1, Pallas kernels: 3.7 us -> 2.58 us  [shards(): call(prompt_kernel, 'prompt', struct((far, ITEM + STAT, HD), BF16), [SMEM...]
  transfers between devices with their start and end apart: 5 -> 3, of which waited for: 2 -> 2; matrix products, arithmetic and copies ran while one was open for 0% -> 0% of each run, Pallas kernels for 1% -> 0%
where the time goes in v4:
time: 96.9 us; the launch traced here: 96.4 us
  blocking collectives  36.9 us (38%)
  starting transfers between devices  30.3 us (31%)
  waiting for transfers between devices  22.2 us (23%)
  Pallas kernels  5.37 us (6%)
    all_to_all x2, blocking collectives, swap(): return lax.all_to_all(array, axes, split_axis=0, concat_axis=0, tiled=True)  36.9 us
    all_to_all x2, starting transfers between devices, swap(): return lax.all_to_all(array, axes, split_axis=0, concat_axis=0, tiled=True)  28 us
    all_to_all x2, waiting for transfers between devices, swap(): return lax.all_to_all(array, axes, split_axis=0, concat_axis=0, tiled=True)  12.1 us
    ppermute x1, waiting for transfers between devices, shards(): there = lax.ppermute(here, NEAR, [(0, 1), (1, 0)])  10.1 us
    pallas_call x1, Pallas kernels, shards(): call(prompt_kernel, 'prompt', struct((far, ITEM + STAT, HD), BF16), [SMEM...  2.58 us
    ppermute x1, starting transfers between devices, shards(): there = lax.ppermute(here, NEAR, [(0, 1), (1, 0)])  2.31 us
  transfers between devices with their start and end apart: 3, of which 2 were waited for; matrix products, arithmetic and copies ran while one was open for 0% of the time, Pallas kernels for 0%

profile of v4, /device:TPU:1, one launch (start us, length us, event | category | flops | bytes accessed | tf_op | source)
XLA Modules:
  0.0 96.4 jit_solution(9552443140551711602)
XLA Ops:
  0.0 0.0 copy-start.5
  0.0 0.7 copy-done.5
  0.7 0.7 spread.1
  1.4 0.0 copy-start.1
  1.4 0.0 copy-start.2
  1.4 0.0 copy-start.7
  1.4 16.6 %all-to-all-start = ((bf16[32,32,128]{2,1,0:T(8,128)(2,1)}), bf16[32,32,128]{2,1,0:T(8,128)(2,1)S(1)}, u32[]{:S(2)}, u32[]{:S(2)}) async-start(bf16[32,32,128]{2,1,0:T(8,128)(2,1)} %spread.1), calls=%async_computation | async-start | bytes 524288 | tf_op jit(solution)/shard_map/all_to_all | solution.py:229
  18.1 0.0 copy-done.1
  18.1 0.0 copy-done.2
  18.1 0.0 copy-done.7
  18.2 2.3 %collective-permute-start = (bf16[1040,128]{1,0:T(8,128)(2,1)S(1)}, bf16[1040,128]{1,0:T(8,128)(2,1)S(1)}, u32[]{:S(2)}, u32[]{:S(2)}) collective-permute-start(bf16[1040,128]{1,0:T(8,128)(2,1)S(1)} %pack.1.refs_0_), channel_id=1, source_target_pairs={{0,8},{8,0},{1,9},{9,1},{2,10},{10,2},{3,11},{11,3},{4,12},{12,4},... | collective-permute-start | bytes 798728 | tf_op jit(solution)/shard_map/ppermute | solution.py:261
  20.5 10.1 %collective-permute-done.refs_1_ = bf16[1040,128]{1,0:T(8,128)(2,1)S(1)} collective-permute-done((bf16[1040,128]{1,0:T(8,128)(2,1)S(1)}, bf16[1040,128]{1,0:T(8,128)(2,1)S(1)}, u32[]{:S(2)}, u32[]{:S(2)}) %collective-permute-start) | collective-permute-done | bytes 266272 | tf_op jit(solution)/shard_map/ppermute | solution.py:261
  30.6 0.0 all-to-all-done.q_ref
  30.6 2.6 %prompt.1 = bf16[32,40,128]{2,1,0:T(8,128)(2,1)} custom-call(s32[1]{0:T(128)} %bitcast.place_ref, bf16[32,32,128]{2,1,0:T(8,128)(2,1)S(1)} %all-to-all-done.q_ref, bf16[1040,128]{1,0:T(8,128)(2,1)S(1)} %pack.1.refs_0_, bf16[1040,128]{1,0:T(8,128)(2,1)S(1)} %collective-permute-done.refs_1_), custom_call_target="tpu_custom_call" | custom-call | tf_op jit(solution)/shard_map/prompt/pallas_call | solution.py:272
  33.2 0.0 copy-start.3
  33.2 0.0 copy-start.4
  33.2 0.0 copy-start.6
  33.2 0.0 copy-start.8
  33.2 0.0 copy-start.9
  33.2 11.3 %all-to-all-start.1 = ((bf16[32,40,128]{2,1,0:T(8,128)(2,1)}), bf16[32,40,128]{2,1,0:T(8,128)(2,1)S(1)}, u32[]{:S(2)}, u32[]{:S(2)}) async-start(bf16[32,40,128]{2,1,0:T(8,128)(2,1)} %prompt.1), calls=%async_computation.1 | async-start | bytes 655360 | tf_op jit(solution)/shard_map/all_to_all | solution.py:229
  44.6 0.0 copy-start
  45.3 0.0 copy-done.3
  45.3 0.0 copy-done.4
  45.3 0.0 copy-done.6
  45.3 0.0 copy-done.8
  45.3 0.0 copy-done.9
  45.3 0.4 own.1
  45.7 12.1 %all-to-all-done.1.part_ref = bf16[32,40,128]{2,1,0:T(8,128)(2,1)S(1)} async-done(((bf16[32,40,128]{2,1,0:T(8,128)(2,1)}), bf16[32,40,128]{2,1,0:T(8,128)(2,1)S(1)}, u32[]{:S(2)}, u32[]{:S(2)}) %all-to-all-start.1) | async-done | bytes 327712 | tf_op jit(solution)/shard_map/all_to_all | solution.py:229
  57.8 0.3 combine.1
  58.1 23.8 %all_to_all.20.x_ref = bf16[64,32,128]{2,1,0:T(8,128)(2,1)S(1)} all-to-all(bf16[64,32,128]{2,1,0:T(8,128)(2,1)S(1)} %combine.1), channel_id=1, replica_groups=mesh['z'=8,'yh'=4,'yl'=2,'head'=8] {'z','yh','yl'}, dimensions={0} | all-to-all | bytes 1048576 | tf_op jit(solution)/shard_map/all_to_all | solution.py:229
  81.9 0.0 copy-done
  81.9 0.8 project.1
  82.7 13.1 %all_to_all.21.x_ref = f32[8,16,256]{2,1,0:T(8,128)S(1)} all-to-all(f32[8,16,256]{2,1,0:T(8,128)S(1)} %project.1), channel_id=1, replica_groups=mesh['z'=8,'yh'=4,'yl'=2,'head'=8] {'head'}, dimensions={0} | all-to-all | bytes 262144 | tf_op jit(solution)/shard_map/all_to_all | solution.py:229
  95.8 0.6 sum.1
  (1 shorter events, 0.0 us)
Async XLA Ops:
  0.0 0.7 copy-start.5
  1.4 16.7 %copy-start.1 = (bf16[512,128]{1,0:T(8,128)(2,1)S(1)}, bf16[512,128]{1,0:T(8,128)(2,1)}, u32[]{:S(2)}) copy-start(bf16[512,128]{1,0:T(8,128)(2,1)} %k_ref.1) | copy-start | bytes 393220
  1.4 16.7 %copy-start.2 = (bf16[512,128]{1,0:T(8,128)(2,1)S(1)}, bf16[512,128]{1,0:T(8,128)(2,1)}, u32[]{:S(2)}) copy-start(bf16[512,128]{1,0:T(8,128)(2,1)} %v_ref.1) | copy-start | bytes 393220
  1.4 16.7 %copy-start.7 = (s32[64,1,8]{0,2,1:T(8,128)S(1)}, s32[64,1,8]{0,2,1:T(8,128)}, u32[]{:S(2)}) copy-start(s32[64,1,8]{0,2,1:T(8,128)} %param.13) | copy-start | bytes 6148
  1.4 29.2 %all-to-all-start = ((bf16[32,32,128]{2,1,0:T(8,128)(2,1)}), bf16[32,32,128]{2,1,0:T(8,128)(2,1)S(1)}, u32[]{:S(2)}, u32[]{:S(2)}) async-start(bf16[32,32,128]{2,1,0:T(8,128)(2,1)} %spread.1), calls=%async_computation | async-start | bytes 524288 | tf_op jit(solution)/shard_map/all_to_all | solution.py:229
  18.2 12.4 %collective-permute-start = (bf16[1040,128]{1,0:T(8,128)(2,1)S(1)}, bf16[1040,128]{1,0:T(8,128)(2,1)S(1)}, u32[]{:S(2)}, u32[]{:S(2)}) collective-permute-start(bf16[1040,128]{1,0:T(8,128)(2,1)S(1)} %pack.1.refs_0_), channel_id=1, source_target_pairs={{0,8},{8,0},{1,9},{9,1},{2,10},{10,2},{3,11},{11,3},{4,12},{12,4},... | collective-permute-start | bytes 798728 | tf_op jit(solution)/shard_map/ppermute | solution.py:261
  33.2 12.1 %copy-start.3 = (bf16[1,256,128]{2,1,0:T(8,128)(2,1)S(1)}, bf16[1,256,128]{2,1,0:T(8,128)(2,1)}, u32[]{:S(2)}) copy-start(bf16[1,256,128]{2,1,0:T(8,128)(2,1)} %param.14) | copy-start | bytes 196612
  33.2 12.1 %copy-start.4 = (bf16[1,256,128]{2,1,0:T(8,128)(2,1)S(1)}, bf16[1,256,128]{2,1,0:T(8,128)(2,1)}, u32[]{:S(2)}) copy-start(bf16[1,256,128]{2,1,0:T(8,128)(2,1)} %param.15) | copy-start | bytes 196612
  33.2 12.1 %copy-start.6 = (bf16[2,1,2048]{2,0,1:T(2,128)(2,1)S(1)}, bf16[2,1,2048]{2,0,1:T(2,128)(2,1)}, u32[]{:S(2)}) copy-start(bf16[2,1,2048]{2,0,1:T(2,128)(2,1)} %param.10) | copy-start | bytes 24580
  33.2 12.1 %copy-start.8 = (bf16[2,1,128]{2,0,1:T(2,128)(2,1)S(1)}, bf16[2,1,128]{2,0,1:T(2,128)(2,1)}, u32[]{:S(2)}) copy-start(bf16[2,1,128]{2,0,1:T(2,128)(2,1)} %param.16) | copy-start | bytes 1540
  33.2 12.1 %copy-start.9 = (bf16[2,1,128]{2,0,1:T(2,128)(2,1)S(1)}, bf16[2,1,128]{2,0,1:T(2,128)(2,1)}, u32[]{:S(2)}) copy-start(bf16[2,1,128]{2,0,1:T(2,128)(2,1)} %param.17) | copy-start | bytes 1540
  33.2 24.6 %all-to-all-start.1 = ((bf16[32,40,128]{2,1,0:T(8,128)(2,1)}), bf16[32,40,128]{2,1,0:T(8,128)(2,1)S(1)}, u32[]{:S(2)}, u32[]{:S(2)}) async-start(bf16[32,40,128]{2,1,0:T(8,128)(2,1)} %prompt.1), calls=%async_computation.1 | async-start | bytes 655360 | tf_op jit(solution)/shard_map/all_to_all | solution.py:229
  44.6 37.3 %copy-start = (bf16[2048,256]{1,0:T(8,128)(2,1)S(1)}, bf16[2048,256]{1,0:T(8,128)(2,1)}, u32[]{:S(2)}) copy-start(bf16[2048,256]{1,0:T(8,128)(2,1)} %w_ref.1) | copy-start | bytes 3145732

commit v5 on v3

--- a/solution.py
+++ b/solution.py
@@ -24,7 +24,7 @@
 
 VMEM = pl.BlockSpec(memory_space=pltpu.VMEM)
 SMEM = pl.BlockSpec(memory_space=pltpu.SMEM)
-PARAMS = pltpu.CompilerParams(vmem_limit_bytes=24 * 1024 * 1024)
+ANY = pl.BlockSpec(memory_space=pl.ANY)
 F32 = jnp.float32
 BF16 = jnp.bfloat16
 
@@ -61,10 +61,16 @@
     out_ref[...] = jnp.broadcast_to(rows[None], out_ref.shape)
 
 
-def pack_kernel(k_ref, v_ref, sel_ref, out_ref):
-    tokens = k_ref.shape[0]
-    out_ref[:tokens, :] = k_ref[...]
-    out_ref[tokens : 2 * tokens, :] = v_ref[...]
+def pack_kernel(k_hbm, v_hbm, sel_hbm, out_ref, sel_ref, sems):
+    tokens = k_hbm.shape[0]
+    copies = [
+        pltpu.make_async_copy(sel_hbm, sel_ref, sems.at[0]),
+        pltpu.make_async_copy(k_hbm, out_ref.at[:tokens], sems.at[1]),
+        pltpu.make_async_copy(v_hbm, out_ref.at[tokens : 2 * tokens], sems.at[2]),
+    ]
+    for copy in copies:
+        copy.start()
+    copies[0].wait()
     slots, samples = sel_ref.shape
     number = iota((FLAG, samples), 0)
     bias = jnp.full((FLAG, samples), NEGATIVE, F32)
@@ -72,6 +78,8 @@
         bias = jnp.where(sel_ref[slot : slot + 1, :] == number, 0.0, bias)
     bias = jnp.concatenate([bias, jnp.zeros((FLAG, HD - samples), F32)], axis=1)
     out_ref[2 * tokens :, :] = bias.astype(BF16)
+    for copy in copies[1:]:
+        copy.wait()
 
 
 def own_kernel(q_ref, ck_ref, cv_ref, nk_ref, nv_ref, pos_ref, out_ref, log_ref, rows_ref):
@@ -102,15 +110,19 @@
     log_ref[...] = jnp.broadcast_to(to_lanes(log_mass, 1), log_ref.shape)
 
 
-def prompt_kernel(place_ref, q_ref, *refs):
+def prompt_kernel(place_ref, own_ref, q_ref, *refs):
     *pack_refs, out_ref, keys_ref = refs
     samples = q_ref.shape[0]
     tokens = (pack_refs[0].shape[0] - FLAG) // 2
-    widen = iota((tokens, FLAG), 0) // BLOCK == iota((tokens, FLAG), 1)
+    widen = iota((FLAG, tokens), 1) // BLOCK == iota((FLAG, tokens), 0)
     widen = widen.astype(F32).astype(BF16)
     for index, ref in enumerate(pack_refs):
-        keys_ref[index, :, :HD] = ref[:tokens, :]
-        keys_ref[index, :, HD:] = dot(widen, ref[2 * tokens :, :]).astype(BF16)
+        place = slice(index * tokens, (index + 1) * tokens)
+        keys_ref[:HD, place] = ref[:tokens, :].T
+        bias = lax.dot_general(
+            ref[2 * tokens :, :], widen, (((0,), (0,)), ((), ())), preferred_element_type=F32
+        )
+        keys_ref[HD:, place] = bias.astype(BF16)
     ones = jnp.ones((tokens, HD), BF16)
     count = TILE * ITEM
     number = iota((count, HD), 0) // ITEM
@@ -118,9 +130,11 @@
         here = slice(first, first + TILE)
         q = q_ref[here].reshape(count, HD)
         sample = (first + number) // 4 * 16 + (first + number) % 4 * 2 + place_ref[0]
-        mine = (iota((count, HD), 1) == sample).astype(F32).astype(BF16)
-        q = jnp.concatenate([q, mine], axis=1)
-        scores = [dot_t(q, keys_ref[index]) for index in range(len(pack_refs))]
+        mine = iota((count, HD), 1) == sample
+        q = jnp.concatenate([q, mine.astype(F32).astype(BF16)], axis=1)
+        scores = []
+        for index in range(len(pack_refs)):
+            scores.append(dot(q, keys_ref[:, index * tokens : (index + 1) * tokens]))
         top = scores[0]
         for score in scores[1:]:
             top = jnp.maximum(top, score)
@@ -207,7 +221,9 @@
     out_ref[...] = total.reshape(out_ref.shape).astype(BF16)
 
 
-def call(kernel, name, out_shape, in_specs, out_specs, scratch=(), flops=0, moved=0):
+def call(
+    kernel, name, out_shape, in_specs, out_specs, scratch=(), flops=0, moved=0, vmem=24
+):
     return pl.pallas_call(
         kernel,
         name=name,
@@ -215,7 +231,7 @@
         in_specs=in_specs,
         out_specs=out_specs,
         scratch_shapes=scratch,
-        compiler_params=PARAMS,
+        compiler_params=pltpu.CompilerParams(vmem_limit_bytes=vmem * 1024 * 1024),
         cost_estimate=pl.CostEstimate(flops=flops, bytes_accessed=moved, transcendentals=0),
     )
 
@@ -249,9 +265,16 @@
     spread = call(
         spread_kernel, "spread", struct((far, ITEM, HD), BF16), [VMEM], VMEM, [rows_scratch]
     )(q)
+    chosen = selected[:, 0, :].T
     here = call(
-        pack_kernel, "pack", struct((2 * tokens + FLAG, HD), BF16), [VMEM] * 3, VMEM
-    )(prompt_keys, prompt_values, selected[:, 0, :].T)
+        pack_kernel,
+        "pack",
+        struct((2 * tokens + FLAG, HD), BF16),
+        [ANY] * 3,
+        VMEM,
+        [pltpu.VMEM(chosen.shape, jnp.int32), pltpu.SemaphoreType.DMA((3,))],
+        vmem=62,
+    )(prompt_keys, prompt_values, chosen)
     gathered = swap(spread, FAR)
     packs = [
         here,
@@ -273,10 +296,10 @@
         prompt_kernel,
         "prompt",
         struct((far, ITEM + STAT, HD), BF16),
-        [SMEM] + [VMEM] * 5,
+        [SMEM, ANY] + [VMEM] * 5,
         VMEM,
-        [pltpu.VMEM((4, tokens, 2 * HD), BF16)],
-    )(place, gathered, *packs)
+        [pltpu.VMEM((2 * HD, 4 * tokens), BF16)],
+    )(place, own, gathered, *packs)
     received = swap(partial, FAR)
     attended = call(
         combine_kernel, "combine", struct((samples, ITEM, HD), BF16), [VMEM] * 3, VMEM

time: 95.1 us -> 92 us (0.967)
  blocking collectives: 34.9 us -> 49.2 us
  waiting for transfers between devices: 21.8 us -> 9.74 us
  starting transfers between devices: 28.2 us -> 24.7 us
  local copies, waits for them, and re-layouts: 2.53 us -> 0.66 us
    all_to_all x2 -> x3, blocking collectives: 34.9 us -> 49.2 us  [swap(): return lax.all_to_all(array, axes, split_axis=0, concat_axis=0, tiled=True)]
    all_to_all x2 -> x1, waiting for transfers between devices: 21.8 us -> 9.73 us  [swap(): return lax.all_to_all(array, axes, split_axis=0, concat_axis=0, tiled=True)]
    ppermute x1, starting transfers between devices: 1.92 us -> 5.84 us  [shards(): lax.ppermute(here, NEAR, [(0, 3), (1, 2), (2, 1), (3, 0)])]
    all_to_all x2 -> x1, starting transfers between devices: 18.3 us -> 14.8 us  [swap(): return lax.all_to_all(array, axes, split_axis=0, concat_axis=0, tiled=True)]
    ppermute x1, starting transfers between devices: 4 us -> 1.92 us  [shards(): lax.ppermute(here, 'zl', [(0, 1), (1, 0)])]
    unnamed x18 -> x14, local copies, waits for them, and re-layouts: 2.53 us -> 0.66 us
    ppermute x1, starting transfers between devices: 4.03 us -> 2.19 us  [shards(): lax.ppermute(here, 'yl', [(0, 1), (1, 0)])]
    pallas_call x1, Pallas kernels: 0.02 us -> 1.73 us  [shards(): call(pack_kernel, 'pack', struct((2 * tokens + FLAG, HD), BF16), [ANY] *...]
  transfers between devices with their start and end apart: 5 -> 4, of which waited for: 2 -> 1; matrix products, arithmetic and copies ran while one was open for 0% -> 0% of each run, Pallas kernels for 1% -> 1%
where the time goes in v5:
time: 92 us; the launch traced here: 91.6 us
  blocking collectives  49.2 us (53%)
  starting transfers between devices  24.7 us (27%)
  waiting for transfers between devices  9.74 us (11%)
  Pallas kernels  6.41 us (7%)
    all_to_all x3, blocking collectives, swap(): return lax.all_to_all(array, axes, split_axis=0, concat_axis=0, tiled=True)  49.2 us
    all_to_all x1, starting transfers between devices, swap(): return lax.all_to_all(array, axes, split_axis=0, concat_axis=0, tiled=True)  14.8 us
    all_to_all x1, waiting for transfers between devices, swap(): return lax.all_to_all(array, axes, split_axis=0, concat_axis=0, tiled=True)  9.73 us
    ppermute x1, starting transfers between devices, shards(): lax.ppermute(here, NEAR, [(0, 3), (1, 2), (2, 1), (3, 0)])  5.84 us
    ppermute x1, starting transfers between devices, shards(): lax.ppermute(here, 'yl', [(0, 1), (1, 0)])  2.19 us
    pallas_call x1, Pallas kernels, shards(): call(prompt_kernel, 'prompt', struct((far, ITEM + STAT, HD), BF16), [SMEM...  2.02 us
    ppermute x1, starting transfers between devices, shards(): lax.ppermute(here, 'zl', [(0, 1), (1, 0)])  1.92 us
  transfers between devices with their start and end apart: 4, of which 1 were waited for; matrix products, arithmetic and copies ran while one was open for 0% of the time, Pallas kernels for 1%

profile of v5, /device:TPU:1, one launch (start us, length us, event | category | flops | bytes accessed | tf_op | source)
XLA Modules:
  0.0 91.6 jit_solution(13130597367911513371)
XLA Ops:
  0.0 0.0 copy-start.4
  0.0 1.7 %pack.1.refs_0_ = bf16[1040,128]{1,0:T(8,128)(2,1)} custom-call(bf16[512,128]{1,0:T(8,128)(2,1)} %k_hbm.1, bf16[512,128]{1,0:T(8,128)(2,1)} %v_hbm.1, s32[8,64]{1,0:T(8,128)} %bitcast.15), custom_call_target="tpu_custom_call" | custom-call | tf_op jit(solution)/shard_map/pack/pallas_call | solution.py:269
  1.7 5.8 %collective-permute-start.2 = (bf16[1040,128]{1,0:T(8,128)(2,1)}, bf16[1040,128]{1,0:T(8,128)(2,1)S(1)}, u32[]{:S(2)}, u32[]{:S(2)}) collective-permute-start(bf16[1040,128]{1,0:T(8,128)(2,1)} %pack.1.refs_0_), channel_id=1, source_target_pairs={{0,72},{8,64},{64,8},{72,0},{1,73},{9,65},{65,9},{73,1},{2,74},{10... | collective-permute-start | bytes 798728 | tf_op jit(solution)/shard_map/ppermute | solution.py:283
  7.6 1.9 %collective-permute-start.1 = (bf16[1040,128]{1,0:T(8,128)(2,1)}, bf16[1040,128]{1,0:T(8,128)(2,1)S(1)}, u32[]{:S(2)}, u32[]{:S(2)}) collective-permute-start(bf16[1040,128]{1,0:T(8,128)(2,1)} %pack.1.refs_0_), channel_id=1, source_target_pairs={{0,64},{64,0},{1,65},{65,1},{2,66},{66,2},{3,67},{67,3},{4,68},{68... | collective-permute-start | bytes 798728 | tf_op jit(solution)/shard_map/ppermute | solution.py:282
  9.5 2.2 %collective-permute-start = (bf16[1040,128]{1,0:T(8,128)(2,1)}, bf16[1040,128]{1,0:T(8,128)(2,1)S(1)}, u32[]{:S(2)}, u32[]{:S(2)}) collective-permute-start(bf16[1040,128]{1,0:T(8,128)(2,1)} %pack.1.refs_0_), channel_id=1, source_target_pairs={{0,8},{8,0},{1,9},{9,1},{2,10},{10,2},{3,11},{11,3},{4,12},{12,4},... | collective-permute-start | bytes 798728 | tf_op jit(solution)/shard_map/ppermute | solution.py:281
  11.7 0.0 copy-done.4
  11.7 0.0 copy-start
  11.7 0.7 spread.1
  12.4 0.0 copy-start.2
  12.4 0.0 copy-start.3
  12.4 14.8 %all-to-all-start = ((bf16[16,32,128]{2,1,0:T(8,128)(2,1)}), bf16[16,32,128]{2,1,0:T(8,128)(2,1)S(1)}, u32[]{:S(2)}, u32[]{:S(2)}) async-start(bf16[16,32,128]{2,1,0:T(8,128)(2,1)} %spread.1), calls=%async_computation | async-start | bytes 262144 | tf_op jit(solution)/shard_map/all_to_all | solution.py:240
  27.8 0.0 copy-start.5
  27.9 0.0 copy-start.6
  27.9 0.0 copy-done.2
  27.9 0.0 copy-done.3
  27.9 0.6 copy-done.5
  28.5 0.0 copy-done.6
  28.5 0.4 own.1
  28.9 9.7 %all-to-all-done.q_ref = bf16[16,32,128]{2,1,0:T(8,128)(2,1)S(1)} async-done(((bf16[16,32,128]{2,1,0:T(8,128)(2,1)}), bf16[16,32,128]{2,1,0:T(8,128)(2,1)S(1)}, u32[]{:S(2)}, u32[]{:S(2)}) %all-to-all-start) | async-done | bytes 131104 | tf_op jit(solution)/shard_map/all_to_all | solution.py:240
  38.6 0.0 collective-permute-done.2.refs_3_
  38.6 0.0 collective-permute-done.1.refs_2_
  38.6 0.0 collective-permute-done.refs_1_
  38.6 0.0 copy-done
  38.6 2.0 %prompt.1 = bf16[16,40,128]{2,1,0:T(8,128)(2,1)S(1)} custom-call(s32[1]{0:T(128)} %bitcast.place_ref, f32[32,128]{1,0:T(8,128)S(1)} %get-tuple-element.7.own_ref, bf16[16,32,128]{2,1,0:T(8,128)(2,1)S(1)} %all-to-all-done.q_ref, bf16[1040,128]{1,0:T(8,128)(2,1)S(1)} %copy-done, bf16[1040,128]{1,0:T(8,128)(2,1)S(1)} %collective-permute-done.refs_1_, ...), custom_call_target="tpu_custom_call" | custom-call | tf_op jit(solution)/shard_map/prompt/pallas_call | solution.py:295
  40.7 0.0 copy-start.1
  40.7 14.7 %all_to_all.20.part_ref = bf16[16,40,128]{2,1,0:T(8,128)(2,1)S(1)} all-to-all(bf16[16,40,128]{2,1,0:T(8,128)(2,1)S(1)} %prompt.1), channel_id=1, replica_groups=mesh['zh'=4,'zl'=2,'yh'=4,'yl'=2,'head'=8] {'zh','yh'}, dimensions={0} | all-to-all | bytes 327680 | tf_op jit(solution)/shard_map/all_to_all | solution.py:240
  55.4 0.2 combine.1
  55.6 19.3 %all_to_all.21.x_ref = bf16[64,32,128]{2,1,0:T(8,128)(2,1)S(1)} all-to-all(bf16[64,32,128]{2,1,0:T(8,128)(2,1)S(1)} %combine.1), channel_id=1, replica_groups=mesh['zh'=4,'zl'=2,'yh'=4,'yl'=2,'head'=8] {'zh','zl','yh','yl'}, dimensions={0} | all-to-all | bytes 1048576 | tf_op jit(solution)/shard_map/all_to_all | solution.py:240
  74.9 0.0 copy-done.1
  74.9 0.8 project.1
  75.7 15.2 %all_to_all.22.x_ref = f32[8,16,256]{2,1,0:T(8,128)S(1)} all-to-all(f32[8,16,256]{2,1,0:T(8,128)S(1)} %project.1), channel_id=1, replica_groups=mesh['zh'=4,'zl'=2,'yh'=4,'yl'=2,'head'=8] {'head'}, dimensions={0} | all-to-all | bytes 262144 | tf_op jit(solution)/shard_map/all_to_all | solution.py:240
  90.9 0.6 sum.1
Async XLA Ops:
  0.0 11.7 %copy-start.4 = (bf16[2,1,2048]{2,0,1:T(2,128)(2,1)S(1)}, bf16[2,1,2048]{2,0,1:T(2,128)(2,1)}, u32[]{:S(2)}) copy-start(bf16[2,1,2048]{2,0,1:T(2,128)(2,1)} %param.10) | copy-start | bytes 24580
  1.7 36.9 %collective-permute-start.2 = (bf16[1040,128]{1,0:T(8,128)(2,1)}, bf16[1040,128]{1,0:T(8,128)(2,1)S(1)}, u32[]{:S(2)}, u32[]{:S(2)}) collective-permute-start(bf16[1040,128]{1,0:T(8,128)(2,1)} %pack.1.refs_0_), channel_id=1, source_target_pairs={{0,72},{8,64},{64,8},{72,0},{1,73},{9,65},{65,9},{73,1},{2,74},{10... | collective-permute-start | bytes 798728 | tf_op jit(solution)/shard_map/ppermute | solution.py:283
  7.6 31.0 %collective-permute-start.1 = (bf16[1040,128]{1,0:T(8,128)(2,1)}, bf16[1040,128]{1,0:T(8,128)(2,1)S(1)}, u32[]{:S(2)}, u32[]{:S(2)}) collective-permute-start(bf16[1040,128]{1,0:T(8,128)(2,1)} %pack.1.refs_0_), channel_id=1, source_target_pairs={{0,64},{64,0},{1,65},{65,1},{2,66},{66,2},{3,67},{67,3},{4,68},{68... | collective-permute-start | bytes 798728 | tf_op jit(solution)/shard_map/ppermute | solution.py:282
  9.5 29.1 %collective-permute-start = (bf16[1040,128]{1,0:T(8,128)(2,1)}, bf16[1040,128]{1,0:T(8,128)(2,1)S(1)}, u32[]{:S(2)}, u32[]{:S(2)}) collective-permute-start(bf16[1040,128]{1,0:T(8,128)(2,1)} %pack.1.refs_0_), channel_id=1, source_target_pairs={{0,8},{8,0},{1,9},{9,1},{2,10},{10,2},{3,11},{11,3},{4,12},{12,4},... | collective-permute-start | bytes 798728 | tf_op jit(solution)/shard_map/ppermute | solution.py:281
  11.7 26.9 %copy-start = (bf16[1040,128]{1,0:T(8,128)(2,1)S(1)}, bf16[1040,128]{1,0:T(8,128)(2,1)}, u32[]{:S(2)}) copy-start(bf16[1040,128]{1,0:T(8,128)(2,1)} %pack.1.refs_0_) | copy-start | bytes 798724
  12.4 15.5 %copy-start.2 = (bf16[1,256,128]{2,1,0:T(8,128)(2,1)S(1)}, bf16[1,256,128]{2,1,0:T(8,128)(2,1)}, u32[]{:S(2)}) copy-start(bf16[1,256,128]{2,1,0:T(8,128)(2,1)} %param.14) | copy-start | bytes 196612
  12.4 15.5 %copy-start.3 = (bf16[1,256,128]{2,1,0:T(8,128)(2,1)S(1)}, bf16[1,256,128]{2,1,0:T(8,128)(2,1)}, u32[]{:S(2)}) copy-start(bf16[1,256,128]{2,1,0:T(8,128)(2,1)} %param.15) | copy-start | bytes 196612
  12.4 26.2 %all-to-all-start = ((bf16[16,32,128]{2,1,0:T(8,128)(2,1)}), bf16[16,32,128]{2,1,0:T(8,128)(2,1)S(1)}, u32[]{:S(2)}, u32[]{:S(2)}) async-start(bf16[16,32,128]{2,1,0:T(8,128)(2,1)} %spread.1), calls=%async_computation | async-start | bytes 262144 | tf_op jit(solution)/shard_map/all_to_all | solution.py:240
  27.8 0.7 copy-start.5
  27.9 0.7 copy-start.6
  40.7 34.3 %copy-start.1 = (bf16[2048,256]{1,0:T(8,128)(2,1)S(1)}, bf16[2048,256]{1,0:T(8,128)(2,1)}, u32[]{:S(2)}) copy-start(bf16[2048,256]{1,0:T(8,128)(2,1)} %w_ref.1) | copy-start | bytes 3145732

commit v6 on v5

--- a/solution.py
+++ b/solution.py
@@ -5,10 +5,10 @@
 from jax import lax
 from jax.experimental import pallas as pl
 from jax.experimental.pallas import tpu as pltpu
-from jax.sharding import Mesh
 from jax.sharding import PartitionSpec as P
 
 HD = 128
+KVH = 8
 PER = 16
 BLOCK = 64
 STEPS = 2
@@ -18,9 +18,10 @@
 NEGATIVE = -1e30
 SCALE = math.log2(math.e) / math.sqrt(HD)
 TILE = 4
-CTX = ("zh", "zl", "yh", "yl")
-FAR = ("zh", "yh")
-NEAR = ("zl", "yl")
+BOTH = ("ctx", "head")
+SIDE = 8
+CORES = 2
+GAP = 2
 
 VMEM = pl.BlockSpec(memory_space=pltpu.VMEM)
 SMEM = pl.BlockSpec(memory_space=pltpu.SMEM)
@@ -126,11 +127,13 @@
     ones = jnp.ones((tokens, HD), BF16)
     count = TILE * ITEM
     number = iota((count, HD), 0) // ITEM
+    lane = iota((count, HD), 1) - place_ref[1]
     for first in range(0, samples, TILE):
         here = slice(first, first + TILE)
         q = q_ref[here].reshape(count, HD)
-        sample = (first + number) // 4 * 16 + (first + number) % 4 * 2 + place_ref[0]
-        mine = iota((count, HD), 1) == sample
+        ring, near = (first + number) // GAP, (first + number) % GAP
+        sample = jnp.where(place_ref[0] == 0, ring * SIDE + near, near * SIDE + ring)
+        mine = lane == sample
         q = jnp.concatenate([q, mine.astype(F32).astype(BF16)], axis=1)
         scores = []
         for index in range(len(pack_refs)):
@@ -236,8 +239,38 @@
     )
 
 
-def swap(array, axes):
-    return lax.all_to_all(array, axes, split_axis=0, concat_axis=0, tiled=True)
+def swap(array, axes, groups=None):
+    return lax.all_to_all(
+        array, axes, split_axis=0, concat_axis=0, axis_index_groups=groups, tiled=True
+    )
+
+
+def device(z, y, head):
+    return (z % SIDE * SIDE + y % SIDE) * KVH + head
+
+
+def far_groups():
+    groups = []
+    for head in range(KVH):
+        for first in range(0, SIDE, GAP):
+            group = []
+            for ring in range(SIDE):
+                for near in range(first, first + GAP):
+                    z, y = (ring, near) if head % CORES == 0 else (near, ring)
+                    group.append(device(z, y, head))
+            groups.append(group)
+    return groups
+
+
+def hops(count):
+    pairs = []
+    for head in range(KVH):
+        for z in range(SIDE):
+            for y in range(SIDE):
+                move = count * GAP
+                target = (z, y + move) if head % CORES == 0 else (z + move, y)
+                pairs.append((device(z, y, head), device(*target, head)))
+    return pairs
 
 
 def shards(
@@ -253,12 +286,16 @@
     out_weight,
 ):
     struct = jax.ShapeDtypeStruct
-    samples = lax.axis_size(CTX)
-    far = lax.axis_size(FAR)
+    samples = lax.axis_size("ctx")
+    far = SIDE * GAP
     heads = lax.axis_size("head")
     tokens = prompt_keys.shape[0]
     columns = out_weight.shape[1]
-    place = (8 * lax.axis_index("zl") + lax.axis_index("yl")).astype(jnp.int32).reshape(1)
+    ctx = lax.axis_index("ctx")
+    odd = lax.axis_index("head") % CORES
+    start = jnp.where(odd == 0, ctx % SIDE // GAP * GAP, ctx // SIDE // GAP * GAP * SIDE)
+    place = jnp.stack([odd, start]).astype(jnp.int32)
+    groups = far_groups()
     rows_scratch = pltpu.VMEM((ITEM, HD), F32)
     q = queries.reshape(STEPS, PER * HD)
 
@@ -275,13 +312,10 @@
         [pltpu.VMEM(chosen.shape, jnp.int32), pltpu.SemaphoreType.DMA((3,))],
         vmem=62,
     )(prompt_keys, prompt_values, chosen)
-    gathered = swap(spread, FAR)
-    packs = [
-        here,
-        lax.ppermute(here, "yl", [(0, 1), (1, 0)]),
-        lax.ppermute(here, "zl", [(0, 1), (1, 0)]),
-        lax.ppermute(here, NEAR, [(0, 3), (1, 2), (2, 1), (3, 0)]),
-    ]
+    gathered = swap(spread, BOTH, groups)
+    packs = [here]
+    for count in range(1, SIDE // GAP):
+        packs.append(lax.ppermute(here, BOTH, hops(count)))
     own, own_log = call(
         own_kernel,
         "own",
@@ -300,11 +334,11 @@
         VMEM,
         [pltpu.VMEM((2 * HD, 4 * tokens), BF16)],
     )(place, own, gathered, *packs)
-    received = swap(partial, FAR)
+    received = swap(partial, BOTH, groups)
     attended = call(
         combine_kernel, "combine", struct((samples, ITEM, HD), BF16), [VMEM] * 3, VMEM
     )(received, own, own_log)
-    every = swap(attended, CTX)
+    every = swap(attended, "ctx")
     product = call(
         project_kernel,
         "project",
@@ -320,19 +354,18 @@
 
 
 def solution(mesh):
-    fine = Mesh(mesh.devices.reshape(4, 2, 4, 2, 8), (*CTX, "head"))
     placed = (
-        P(None, CTX, "head"),
-        P(CTX, "head"),
-        P(CTX, "head"),
-        P(None, "head", CTX),
-        P(CTX, None, "head"),
-        P(CTX, None, "head"),
-        P(None, CTX, "head"),
-        P(None, CTX, "head"),
-        P(CTX),
-        P("head", CTX),
+        P(None, "ctx", "head"),
+        P("ctx", "head"),
+        P("ctx", "head"),
+        P(None, "head", "ctx"),
+        P("ctx", None, "head"),
+        P("ctx", None, "head"),
+        P(None, "ctx", "head"),
+        P(None, "ctx", "head"),
+        P("ctx"),
+        P("head", "ctx"),
     )
     return jax.shard_map(
-        shards, mesh=fine, in_specs=placed, out_specs=P(None, "head", CTX), check_vma=False
-    )
+        shards, mesh=mesh, in_specs=placed, out_specs=P(None, "head", "ctx"), check_vma=False
+    )

time: 92 us -> 91.3 us (level)
  waiting for transfers between devices: 9.74 us -> 7.13 us
    ppermute x3, starting transfers between devices: 9.95 us -> 17.6 us  [shards(): packs.append(lax.ppermute(here, BOTH, hops(count)))]
    all_to_all x1, starting transfers between devices: 14.8 us -> 7.97 us  [swap(): lax.all_to_all(array, axes, split_axis=0, concat_axis=0, axis_index_group...]
    all_to_all x1, waiting for transfers between devices: 9.73 us -> 7.12 us  [swap(): lax.all_to_all(array, axes, split_axis=0, concat_axis=0, axis_index_group...]
where the time goes in v6:
time: 91.3 us; the launch traced here: 90.8 us
  blocking collectives  50 us (55%)
  starting transfers between devices  25.6 us (28%)
  waiting for transfers between devices  7.13 us (8%)
  Pallas kernels  6.96 us (8%)
    all_to_all x3, blocking collectives, swap(): lax.all_to_all(array, axes, split_axis=0, concat_axis=0, axis_index_group...  50 us
    ppermute x3, starting transfers between devices, shards(): packs.append(lax.ppermute(here, BOTH, hops(count)))  17.6 us
    all_to_all x1, starting transfers between devices, swap(): lax.all_to_all(array, axes, split_axis=0, concat_axis=0, axis_index_group...  7.97 us
    all_to_all x1, waiting for transfers between devices, swap(): lax.all_to_all(array, axes, split_axis=0, concat_axis=0, axis_index_group...  7.12 us
    pallas_call x1, Pallas kernels, shards(): call(prompt_kernel, 'prompt', struct((far, ITEM + STAT, HD), BF16), [SMEM...  2.57 us
  transfers between devices with their start and end apart: 4, of which 1 were waited for; matrix products, arithmetic and copies ran while one was open for 0% of the time, Pallas kernels for 1%

profile of v6, /device:TPU:1, one launch (start us, length us, event | category | flops | bytes accessed | tf_op | source)
XLA Modules:
  0.0 90.8 jit_solution(17970048019229585713)
XLA Ops:
  0.0 0.0 copy-start.4
  0.0 1.7 %pack.1.refs_0_ = bf16[1040,128]{1,0:T(8,128)(2,1)} custom-call(bf16[512,128]{1,0:T(8,128)(2,1)} %k_hbm.1, bf16[512,128]{1,0:T(8,128)(2,1)} %v_hbm.1, s32[8,64]{1,0:T(8,128)} %bitcast.16), custom_call_target="tpu_custom_call" | custom-call | tf_op jit(solution)/shard_map/pack/pallas_call | solution.py:306
  1.7 11.5 %collective-permute-start.2 = (bf16[1040,128]{1,0:T(8,128)(2,1)}, bf16[1040,128]{1,0:T(8,128)(2,1)S(1)}, u32[]{:S(2)}, u32[]{:S(2)}) collective-permute-start(bf16[1040,128]{1,0:T(8,128)(2,1)} %pack.1.refs_0_), channel_id=1, source_target_pairs={{0,48},{8,56},{16,0},{24,8},{32,16},{40,24},{48,32},{56,40},{64,11... | collective-permute-start | bytes 798728 | tf_op jit(solution)/shard_map/ppermute | solution.py:318
  13.2 1.9 %collective-permute-start.1 = (bf16[1040,128]{1,0:T(8,128)(2,1)}, bf16[1040,128]{1,0:T(8,128)(2,1)S(1)}, u32[]{:S(2)}, u32[]{:S(2)}) collective-permute-start(bf16[1040,128]{1,0:T(8,128)(2,1)} %pack.1.refs_0_), channel_id=1, source_target_pairs={{0,32},{8,40},{16,48},{24,56},{32,0},{40,8},{48,16},{56,24},{64,96... | collective-permute-start | bytes 798728 | tf_op jit(solution)/shard_map/ppermute | solution.py:318
  15.2 4.2 %collective-permute-start = (bf16[1040,128]{1,0:T(8,128)(2,1)}, bf16[1040,128]{1,0:T(8,128)(2,1)S(1)}, u32[]{:S(2)}, u32[]{:S(2)}) collective-permute-start(bf16[1040,128]{1,0:T(8,128)(2,1)} %pack.1.refs_0_), channel_id=1, source_target_pairs={{0,16},{8,24},{16,32},{24,40},{32,48},{40,56},{48,0},{56,8},{64,80... | collective-permute-start | bytes 798728 | tf_op jit(solution)/shard_map/ppermute | solution.py:318
  19.4 0.0 copy-done.4
  19.4 0.7 spread.1
  20.1 0.0 copy-start
  20.1 8.0 %all-to-all-start = ((bf16[16,32,128]{2,1,0:T(8,128)(2,1)}), bf16[16,32,128]{2,1,0:T(8,128)(2,1)S(1)}, u32[]{:S(2)}, u32[]{:S(2)}) async-start(bf16[16,32,128]{2,1,0:T(8,128)(2,1)} %spread.1), calls=%async_computation | async-start | bytes 262144 | tf_op jit(solution)/shard_map/all_to_all | solution.py:243
  28.1 0.0 copy-start.5
  28.1 0.0 copy-start.6
  28.1 0.0 copy-start.2
  28.1 0.0 copy-start.3
  28.8 0.0 copy-done.5
  28.8 0.0 copy-done.6
  28.9 0.1 copy-done.2
  28.9 0.0 copy-done.3
  29.0 0.4 own.1
  29.3 0.1 pad_add_fusion.place_ref
  29.4 7.1 %all-to-all-done.q_ref = bf16[16,32,128]{2,1,0:T(8,128)(2,1)S(1)} async-done(((bf16[16,32,128]{2,1,0:T(8,128)(2,1)}), bf16[16,32,128]{2,1,0:T(8,128)(2,1)S(1)}, u32[]{:S(2)}, u32[]{:S(2)}) %all-to-all-start) | async-done | bytes 131104 | tf_op jit(solution)/shard_map/all_to_all | solution.py:243
  36.5 0.0 collective-permute-done.2.refs_3_
  36.5 0.0 collective-permute-done.1.refs_2_
  36.5 0.0 collective-permute-done.refs_1_
  36.5 0.0 copy-done
  36.6 2.6 %prompt.1 = bf16[16,40,128]{2,1,0:T(8,128)(2,1)S(1)} custom-call(s32[2]{0:T(128)S(1)} %pad_add_fusion.place_ref, f32[32,128]{1,0:T(8,128)S(1)} %get-tuple-element.7.own_ref, bf16[16,32,128]{2,1,0:T(8,128)(2,1)S(1)} %all-to-all-done.q_ref, bf16[1040,128]{1,0:T(8,128)(2,1)S(1)} %copy-done, bf16[1040,128]{1,0:T(8,128)(2,1)S(1)} %collective-permute-done.refs_1_, ...), custom_call_target="tpu_custom_call" | custom-call | tf_op jit(solution)/shard_map/prompt/pallas_call | solution.py:329
  39.1 0.0 copy-start.1
  39.1 12.2 %all_to_all.20.part_ref = bf16[16,40,128]{2,1,0:T(8,128)(2,1)S(1)} all-to-all(bf16[16,40,128]{2,1,0:T(8,128)(2,1)S(1)} %prompt.1), channel_id=1, replica_groups={{0,8,64,72,128,136,192,200,256,264,320,328,384,392,448,456},{16,24,80,8..., dimensions={0} | all-to-all | bytes 327680 | tf_op jit(solution)/shard_map/all_to_all | solution.py:243
  51.4 0.2 combine.1
  51.6 24.4 %all_to_all.21.x_ref = bf16[64,32,128]{2,1,0:T(8,128)(2,1)S(1)} all-to-all(bf16[64,32,128]{2,1,0:T(8,128)(2,1)S(1)} %combine.1), channel_id=1, replica_groups=mesh['ctx'=64,'head'=8] {'ctx'}, dimensions={0} | all-to-all | bytes 1048576 | tf_op jit(solution)/shard_map/all_to_all | solution.py:243
  76.0 0.0 copy-done.1
  76.0 0.8 project.1
  76.8 13.4 %all_to_all.22.x_ref = f32[8,16,256]{2,1,0:T(8,128)S(1)} all-to-all(f32[8,16,256]{2,1,0:T(8,128)S(1)} %project.1), channel_id=1, replica_groups=mesh['ctx'=64,'head'=8] {'head'}, dimensions={0} | all-to-all | bytes 262144 | tf_op jit(solution)/shard_map/all_to_all | solution.py:243
  90.2 0.6 sum.1
Async XLA Ops:
  0.0 19.4 %copy-start.4 = (bf16[2,1,2048]{2,0,1:T(2,128)(2,1)S(1)}, bf16[2,1,2048]{2,0,1:T(2,128)(2,1)}, u32[]{:S(2)}) copy-start(bf16[2,1,2048]{2,0,1:T(2,128)(2,1)} %param.10) | copy-start | bytes 24580
  1.7 34.8 %collective-permute-start.2 = (bf16[1040,128]{1,0:T(8,128)(2,1)}, bf16[1040,128]{1,0:T(8,128)(2,1)S(1)}, u32[]{:S(2)}, u32[]{:S(2)}) collective-permute-start(bf16[1040,128]{1,0:T(8,128)(2,1)} %pack.1.refs_0_), channel_id=1, source_target_pairs={{0,48},{8,56},{16,0},{24,8},{32,16},{40,24},{48,32},{56,40},{64,11... | collective-permute-start | bytes 798728 | tf_op jit(solution)/shard_map/ppermute | solution.py:318
  13.2 23.3 %collective-permute-start.1 = (bf16[1040,128]{1,0:T(8,128)(2,1)}, bf16[1040,128]{1,0:T(8,128)(2,1)S(1)}, u32[]{:S(2)}, u32[]{:S(2)}) collective-permute-start(bf16[1040,128]{1,0:T(8,128)(2,1)} %pack.1.refs_0_), channel_id=1, source_target_pairs={{0,32},{8,40},{16,48},{24,56},{32,0},{40,8},{48,16},{56,24},{64,96... | collective-permute-start | bytes 798728 | tf_op jit(solution)/shard_map/ppermute | solution.py:318
  15.2 21.4 %collective-permute-start = (bf16[1040,128]{1,0:T(8,128)(2,1)}, bf16[1040,128]{1,0:T(8,128)(2,1)S(1)}, u32[]{:S(2)}, u32[]{:S(2)}) collective-permute-start(bf16[1040,128]{1,0:T(8,128)(2,1)} %pack.1.refs_0_), channel_id=1, source_target_pairs={{0,16},{8,24},{16,32},{24,40},{32,48},{40,56},{48,0},{56,8},{64,80... | collective-permute-start | bytes 798728 | tf_op jit(solution)/shard_map/ppermute | solution.py:318
  20.1 16.5 %copy-start = (bf16[1040,128]{1,0:T(8,128)(2,1)S(1)}, bf16[1040,128]{1,0:T(8,128)(2,1)}, u32[]{:S(2)}) copy-start(bf16[1040,128]{1,0:T(8,128)(2,1)} %pack.1.refs_0_) | copy-start | bytes 798724
  20.1 16.4 %all-to-all-start = ((bf16[16,32,128]{2,1,0:T(8,128)(2,1)}), bf16[16,32,128]{2,1,0:T(8,128)(2,1)S(1)}, u32[]{:S(2)}, u32[]{:S(2)}) async-start(bf16[16,32,128]{2,1,0:T(8,128)(2,1)} %spread.1), calls=%async_computation | async-start | bytes 262144 | tf_op jit(solution)/shard_map/all_to_all | solution.py:243
  28.1 0.8 copy-start.5
  28.1 0.8 copy-start.6
  28.1 0.8 copy-start.2
  28.1 0.9 copy-start.3
  39.1 36.9 %copy-start.1 = (bf16[2048,256]{1,0:T(8,128)(2,1)S(1)}, bf16[2048,256]{1,0:T(8,128)(2,1)}, u32[]{:S(2)}) copy-start(bf16[2048,256]{1,0:T(8,128)(2,1)} %w_ref.1) | copy-start | bytes 3145732

commit v7 on v6

--- a/solution.py
+++ b/solution.py
@@ -57,21 +57,22 @@
     return jnp.sum(jnp.where(pick, column.reshape(shape), 0.0), axis=1)
 
 
-def spread_kernel(q_ref, out_ref, rows_ref):
-    rows = item_rows(q_ref, rows_ref).astype(BF16)
-    out_ref[...] = jnp.broadcast_to(rows[None], out_ref.shape)
-
-
-def pack_kernel(k_hbm, v_hbm, sel_hbm, out_ref, sel_ref, sems):
+def pack_kernel(
+    q_hbm, k_hbm, v_hbm, sel_hbm, spread_ref, out_ref, q_ref, sel_ref, rows_ref, sems
+):
     tokens = k_hbm.shape[0]
     copies = [
-        pltpu.make_async_copy(sel_hbm, sel_ref, sems.at[0]),
-        pltpu.make_async_copy(k_hbm, out_ref.at[:tokens], sems.at[1]),
-        pltpu.make_async_copy(v_hbm, out_ref.at[tokens : 2 * tokens], sems.at[2]),
+        pltpu.make_async_copy(q_hbm, q_ref, sems.at[0]),
+        pltpu.make_async_copy(sel_hbm, sel_ref, sems.at[1]),
+        pltpu.make_async_copy(k_hbm, out_ref.at[:tokens], sems.at[2]),
+        pltpu.make_async_copy(v_hbm, out_ref.at[tokens : 2 * tokens], sems.at[3]),
     ]
     for copy in copies:
         copy.start()
     copies[0].wait()
+    rows = item_rows(q_ref, rows_ref).astype(BF16)
+    spread_ref[...] = jnp.broadcast_to(rows[None], spread_ref.shape)
+    copies[1].wait()
     slots, samples = sel_ref.shape
     number = iota((FLAG, samples), 0)
     bias = jnp.full((FLAG, samples), NEGATIVE, F32)
@@ -79,7 +80,7 @@
         bias = jnp.where(sel_ref[slot : slot + 1, :] == number, 0.0, bias)
     bias = jnp.concatenate([bias, jnp.zeros((FLAG, HD - samples), F32)], axis=1)
     out_ref[2 * tokens :, :] = bias.astype(BF16)
-    for copy in copies[1:]:
+    for copy in copies[2:]:
         copy.wait()
 
 
@@ -127,13 +128,14 @@
     ones = jnp.ones((tokens, HD), BF16)
     count = TILE * ITEM
     number = iota((count, HD), 0) // ITEM
-    lane = iota((count, HD), 1) - place_ref[1]
+    ring, near = number // GAP, number % GAP
+    odd, start = place_ref[0] // (SIDE * SIDE), place_ref[0] % (SIDE * SIDE)
+    sample = jnp.where(odd == 0, ring * SIDE + near, near * SIDE + ring)
+    lane = iota((count, HD), 1) - sample
     for first in range(0, samples, TILE):
         here = slice(first, first + TILE)
         q = q_ref[here].reshape(count, HD)
-        ring, near = (first + number) // GAP, (first + number) % GAP
-        sample = jnp.where(place_ref[0] == 0, ring * SIDE + near, near * SIDE + ring)
-        mine = lane == sample
+        mine = lane == start + first // GAP * jnp.where(odd == 0, SIDE, 1)
         q = jnp.concatenate([q, mine.astype(F32).astype(BF16)], axis=1)
         scores = []
         for index in range(len(pack_refs)):
@@ -294,24 +296,26 @@
     ctx = lax.axis_index("ctx")
     odd = lax.axis_index("head") % CORES
     start = jnp.where(odd == 0, ctx % SIDE // GAP * GAP, ctx // SIDE // GAP * GAP * SIDE)
-    place = jnp.stack([odd, start]).astype(jnp.int32)
+    place = (odd * (SIDE * SIDE) + start).astype(jnp.int32).reshape(1)
     groups = far_groups()
     rows_scratch = pltpu.VMEM((ITEM, HD), F32)
     q = queries.reshape(STEPS, PER * HD)
 
-    spread = call(
-        spread_kernel, "spread", struct((far, ITEM, HD), BF16), [VMEM], VMEM, [rows_scratch]
-    )(q)
     chosen = selected[:, 0, :].T
-    here = call(
+    spread, here = call(
         pack_kernel,
         "pack",
-        struct((2 * tokens + FLAG, HD), BF16),
-        [ANY] * 3,
-        VMEM,
-        [pltpu.VMEM(chosen.shape, jnp.int32), pltpu.SemaphoreType.DMA((3,))],
+        (struct((far, ITEM, HD), BF16), struct((2 * tokens + FLAG, HD), BF16)),
+        [ANY] * 4,
+        (VMEM, VMEM),
+        [
+            pltpu.VMEM(q.shape, BF16),
+            pltpu.VMEM(chosen.shape, jnp.int32),
+            rows_scratch,
+            pltpu.SemaphoreType.DMA((4,)),
+        ],
         vmem=62,
-    )(prompt_keys, prompt_values, chosen)
+    )(q, prompt_keys, prompt_values, chosen)
     gathered = swap(spread, BOTH, groups)
     packs = [here]
     for count in range(1, SIDE // GAP):

time: 91.3 us -> 90.1 us (0.987)
  Pallas kernels: 6.96 us -> 5.8 us
    pallas_call x2 -> x1, Pallas kernels: 2.4 us -> 1.8 us  [shards(): call(pack_kernel, 'pack', (struct((far, ITEM, HD), BF16), struct((2 * tok...]
  transfers between devices with their start and end apart: 4 -> 4, of which waited for: 1 -> 1; matrix products, arithmetic and copies ran while one was open for 0% -> 0% of each run, Pallas kernels for 1% -> 0%
where the time goes in v7:
time: 90.1 us; the launch traced here: 89.7 us
  blocking collectives  50 us (55%)
  starting transfers between devices  25.6 us (28%)
  waiting for transfers between devices  7.19 us (8%)
  Pallas kernels  5.8 us (6%)
    all_to_all x3, blocking collectives, swap(): lax.all_to_all(array, axes, split_axis=0, concat_axis=0, axis_index_group...  50 us
    ppermute x3, starting transfers between devices, shards(): packs.append(lax.ppermute(here, BOTH, hops(count)))  17.6 us
    all_to_all x1, starting transfers between devices, swap(): lax.all_to_all(array, axes, split_axis=0, concat_axis=0, axis_index_group...  7.98 us
    all_to_all x1, waiting for transfers between devices, swap(): lax.all_to_all(array, axes, split_axis=0, concat_axis=0, axis_index_group...  7.18 us
    pallas_call x1, Pallas kernels, shards(): call(prompt_kernel, 'prompt', struct((far, ITEM + STAT, HD), BF16), [SMEM...  2.02 us
  transfers between devices with their start and end apart: 4, of which 1 were waited for; matrix products, arithmetic and copies ran while one was open for 0% of the time, Pallas kernels for 0%

profile of v7, /device:TPU:1, one launch (start us, length us, event | category | flops | bytes accessed | tf_op | source)
XLA Modules:
  0.0 89.7 jit_solution(11147563107500813802)
XLA Ops:
  0.0 1.8 %pack.1 = (bf16[16,32,128]{2,1,0:T(8,128)(2,1)}, bf16[1040,128]{1,0:T(8,128)(2,1)}) custom-call(bf16[2,2048]{1,0:T(2,128)(2,1)} %bitcast.11, bf16[512,128]{1,0:T(8,128)(2,1)} %k_hbm.1, bf16[512,128]{1,0:T(8,128)(2,1)} %v_hbm.1, s32[8,64]{1,0:T(8,128)} %bitcast.15), custom_call_target="tpu_custom_call" | custom-call | tf_op jit(solution)/shard_map/pack/pallas_call | solution.py:305
  1.8 11.5 %collective-permute-start.2 = (bf16[1040,128]{1,0:T(8,128)(2,1)}, bf16[1040,128]{1,0:T(8,128)(2,1)S(1)}, u32[]{:S(2)}, u32[]{:S(2)}) collective-permute-start(bf16[1040,128]{1,0:T(8,128)(2,1)} %get-tuple-element.11.refs_0_), channel_id=1, source_target_pairs={{0,48},{8,56},{16,0},{24,8},{32,16},{40,24},{48,32},{56,40},{64,11... | collective-permute-start | bytes 798728 | tf_op jit(solution)/shard_map/ppermute | solution.py:322
  13.3 1.9 %collective-permute-start.1 = (bf16[1040,128]{1,0:T(8,128)(2,1)}, bf16[1040,128]{1,0:T(8,128)(2,1)S(1)}, u32[]{:S(2)}, u32[]{:S(2)}) collective-permute-start(bf16[1040,128]{1,0:T(8,128)(2,1)} %get-tuple-element.11.refs_0_), channel_id=1, source_target_pairs={{0,32},{8,40},{16,48},{24,56},{32,0},{40,8},{48,16},{56,24},{64,96... | collective-permute-start | bytes 798728 | tf_op jit(solution)/shard_map/ppermute | solution.py:322
  15.2 4.2 %collective-permute-start = (bf16[1040,128]{1,0:T(8,128)(2,1)}, bf16[1040,128]{1,0:T(8,128)(2,1)S(1)}, u32[]{:S(2)}, u32[]{:S(2)}) collective-permute-start(bf16[1040,128]{1,0:T(8,128)(2,1)} %get-tuple-element.11.refs_0_), channel_id=1, source_target_pairs={{0,16},{8,24},{16,32},{24,40},{32,48},{40,56},{48,0},{56,8},{64,80... | collective-permute-start | bytes 798728 | tf_op jit(solution)/shard_map/ppermute | solution.py:322
  19.5 0.0 copy-start.1
  19.5 8.0 %all-to-all-start = ((bf16[16,32,128]{2,1,0:T(8,128)(2,1)}), bf16[16,32,128]{2,1,0:T(8,128)(2,1)S(1)}, u32[]{:S(2)}, u32[]{:S(2)}) async-start(bf16[16,32,128]{2,1,0:T(8,128)(2,1)} %get-tuple-element.10), calls=%async_computation | async-start | bytes 262144 | tf_op jit(solution)/shard_map/all_to_all | solution.py:245
  27.5 0.0 copy-start.4
  27.5 0.0 copy-start.5
  27.5 0.0 copy-start.6
  27.5 0.0 copy-start.2
  27.5 0.0 copy-start.3
  28.3 0.0 copy-done.4
  28.3 0.0 copy-done.5
  28.3 0.0 copy-done.6
  28.3 0.1 copy-done.2
  28.4 0.0 copy-done.3
  28.4 0.4 own.1
  28.8 7.2 %all-to-all-done.q_ref = bf16[16,32,128]{2,1,0:T(8,128)(2,1)S(1)} async-done(((bf16[16,32,128]{2,1,0:T(8,128)(2,1)}), bf16[16,32,128]{2,1,0:T(8,128)(2,1)S(1)}, u32[]{:S(2)}, u32[]{:S(2)}) %all-to-all-start) | async-done | bytes 131104 | tf_op jit(solution)/shard_map/all_to_all | solution.py:245
  35.9 0.0 collective-permute-done.2.refs_3_
  35.9 0.0 collective-permute-done.1.refs_2_
  35.9 0.0 collective-permute-done.refs_1_
  36.0 0.0 copy-done.1
  36.0 2.0 %prompt.1 = bf16[16,40,128]{2,1,0:T(8,128)(2,1)S(1)} custom-call(s32[1]{0:T(128)} %bitcast.place_ref, f32[32,128]{1,0:T(8,128)S(1)} %get-tuple-element.9.own_ref, bf16[16,32,128]{2,1,0:T(8,128)(2,1)S(1)} %all-to-all-done.q_ref, bf16[1040,128]{1,0:T(8,128)(2,1)S(1)} %copy-done.1, bf16[1040,128]{1,0:T(8,128)(2,1)S(1)} %collective-permute-done.refs_1_, ...), custom_call_target="tpu_custom_call" | custom-call | tf_op jit(solution)/shard_map/prompt/pallas_call | solution.py:333
  38.0 0.0 copy-start
  38.0 13.0 %all_to_all.20.part_ref = bf16[16,40,128]{2,1,0:T(8,128)(2,1)S(1)} all-to-all(bf16[16,40,128]{2,1,0:T(8,128)(2,1)S(1)} %prompt.1), channel_id=1, replica_groups={{0,8,64,72,128,136,192,200,256,264,320,328,384,392,448,456},{16,24,80,8..., dimensions={0} | all-to-all | bytes 327680 | tf_op jit(solution)/shard_map/all_to_all | solution.py:245
  51.0 0.2 combine.1
  51.2 22.6 %all_to_all.21.x_ref = bf16[64,32,128]{2,1,0:T(8,128)(2,1)S(1)} all-to-all(bf16[64,32,128]{2,1,0:T(8,128)(2,1)S(1)} %combine.1), channel_id=1, replica_groups=mesh['ctx'=64,'head'=8] {'ctx'}, dimensions={0} | all-to-all | bytes 1048576 | tf_op jit(solution)/shard_map/all_to_all | solution.py:245
  73.8 0.0 copy-done
  73.8 0.8 project.1
  74.6 14.5 %all_to_all.22.x_ref = f32[8,16,256]{2,1,0:T(8,128)S(1)} all-to-all(f32[8,16,256]{2,1,0:T(8,128)S(1)} %project.1), channel_id=1, replica_groups=mesh['ctx'=64,'head'=8] {'head'}, dimensions={0} | all-to-all | bytes 262144 | tf_op jit(solution)/shard_map/all_to_all | solution.py:245
  89.1 0.6 sum.1
Async XLA Ops:
  1.8 34.1 %collective-permute-start.2 = (bf16[1040,128]{1,0:T(8,128)(2,1)}, bf16[1040,128]{1,0:T(8,128)(2,1)S(1)}, u32[]{:S(2)}, u32[]{:S(2)}) collective-permute-start(bf16[1040,128]{1,0:T(8,128)(2,1)} %get-tuple-element.11.refs_0_), channel_id=1, source_target_pairs={{0,48},{8,56},{16,0},{24,8},{32,16},{40,24},{48,32},{56,40},{64,11... | collective-permute-start | bytes 798728 | tf_op jit(solution)/shard_map/ppermute | solution.py:322
  13.3 22.6 %collective-permute-start.1 = (bf16[1040,128]{1,0:T(8,128)(2,1)}, bf16[1040,128]{1,0:T(8,128)(2,1)S(1)}, u32[]{:S(2)}, u32[]{:S(2)}) collective-permute-start(bf16[1040,128]{1,0:T(8,128)(2,1)} %get-tuple-element.11.refs_0_), channel_id=1, source_target_pairs={{0,32},{8,40},{16,48},{24,56},{32,0},{40,8},{48,16},{56,24},{64,96... | collective-permute-start | bytes 798728 | tf_op jit(solution)/shard_map/ppermute | solution.py:322
  15.2 20.7 %collective-permute-start = (bf16[1040,128]{1,0:T(8,128)(2,1)}, bf16[1040,128]{1,0:T(8,128)(2,1)S(1)}, u32[]{:S(2)}, u32[]{:S(2)}) collective-permute-start(bf16[1040,128]{1,0:T(8,128)(2,1)} %get-tuple-element.11.refs_0_), channel_id=1, source_target_pairs={{0,16},{8,24},{16,32},{24,40},{32,48},{40,56},{48,0},{56,8},{64,80... | collective-permute-start | bytes 798728 | tf_op jit(solution)/shard_map/ppermute | solution.py:322
  19.5 16.5 %copy-start.1 = (bf16[1040,128]{1,0:T(8,128)(2,1)S(1)}, bf16[1040,128]{1,0:T(8,128)(2,1)}, u32[]{:S(2)}) copy-start(bf16[1040,128]{1,0:T(8,128)(2,1)} %get-tuple-element.11.refs_0_) | copy-start | bytes 798724
  19.5 16.5 %all-to-all-start = ((bf16[16,32,128]{2,1,0:T(8,128)(2,1)}), bf16[16,32,128]{2,1,0:T(8,128)(2,1)S(1)}, u32[]{:S(2)}, u32[]{:S(2)}) async-start(bf16[16,32,128]{2,1,0:T(8,128)(2,1)} %get-tuple-element.10), calls=%async_computation | async-start | bytes 262144 | tf_op jit(solution)/shard_map/all_to_all | solution.py:245
  27.5 0.8 copy-start.4
  27.5 0.8 copy-start.5
  27.5 0.8 copy-start.6
  27.5 0.9 copy-start.2
  27.5 0.9 copy-start.3
  38.0 35.8 %copy-start = (bf16[2048,256]{1,0:T(8,128)(2,1)S(1)}, bf16[2048,256]{1,0:T(8,128)(2,1)}, u32[]{:S(2)}) copy-start(bf16[2048,256]{1,0:T(8,128)(2,1)} %w_ref.1) | copy-start | bytes 3145732

commit v8 on v7

--- a/solution.py
+++ b/solution.py
@@ -201,11 +201,17 @@
     out_ref[...] = jnp.broadcast_to(attended[None], out_ref.shape)
 
 
+def peer_sample(peer):
+    return peer * 11 % (SIDE * SIDE)
+
+
 def project_kernel(x_ref, w_ref, out_ref, rows_ref):
     samples = x_ref.shape[0]
     parts = out_ref.shape[0]
     per_part = samples // parts
-    rows_ref[...] = x_ref[...].reshape(samples * ITEM, HD).astype(F32)
+    for peer in range(samples):
+        start = peer_sample(peer) * ITEM
+        rows_ref[start : start + ITEM, :] = x_ref[peer].astype(F32)
     columns = []
     for head in range(PER):
         pieces = [
@@ -262,6 +268,12 @@
                     group.append(device(z, y, head))
             groups.append(group)
     return groups
+
+
+def all_groups():
+    return [
+        [peer_sample(peer) * KVH + head for peer in range(SIDE * SIDE)] for head in range(KVH)
+    ]
 
 
 def hops(count):
@@ -342,7 +354,7 @@
     attended = call(
         combine_kernel, "combine", struct((samples, ITEM, HD), BF16), [VMEM] * 3, VMEM
     )(received, own, own_log)
-    every = swap(attended, "ctx")
+    every = swap(attended, BOTH, all_groups())
     product = call(
         project_kernel,
         "project",

time: 90.1 us -> 89.6 us (level)
  no operation moved by 1% of the time
where the time goes in v8:
time: 89.6 us; the launch traced here: 88.8 us
  blocking collectives  49.2 us (55%)
  starting transfers between devices  25.6 us (29%)
  waiting for transfers between devices  7.19 us (8%)
  Pallas kernels  5.81 us (6%)
    all_to_all x3, blocking collectives, swap(): lax.all_to_all(array, axes, split_axis=0, concat_axis=0, axis_index_group...  49.2 us
    ppermute x3, starting transfers between devices, shards(): packs.append(lax.ppermute(here, BOTH, hops(count)))  17.6 us
    all_to_all x1, starting transfers between devices, swap(): lax.all_to_all(array, axes, split_axis=0, concat_axis=0, axis_index_group...  7.98 us
    all_to_all x1, waiting for transfers between devices, swap(): lax.all_to_all(array, axes, split_axis=0, concat_axis=0, axis_index_group...  7.18 us
    pallas_call x1, Pallas kernels, shards(): call(prompt_kernel, 'prompt', struct((far, ITEM + STAT, HD), BF16), [SMEM...  2.02 us
    pallas_call x1, Pallas kernels, shards(): call(pack_kernel, 'pack', (struct((far, ITEM, HD), BF16), struct((2 * tok...  1.8 us
  transfers between devices with their start and end apart: 4, of which 1 were waited for; matrix products, arithmetic and copies ran while one was open for 0% of the time, Pallas kernels for 0%

profile of v8, /device:TPU:1, one launch (start us, length us, event | category | flops | bytes accessed | tf_op | source)
XLA Modules:
  0.0 88.8 jit_solution(15167703977703121870)
XLA Ops:
  0.0 1.8 %pack.1 = (bf16[16,32,128]{2,1,0:T(8,128)(2,1)}, bf16[1040,128]{1,0:T(8,128)(2,1)}) custom-call(bf16[2,2048]{1,0:T(2,128)(2,1)} %bitcast.11, bf16[512,128]{1,0:T(8,128)(2,1)} %k_hbm.1, bf16[512,128]{1,0:T(8,128)(2,1)} %v_hbm.1, s32[8,64]{1,0:T(8,128)} %bitcast.15), custom_call_target="tpu_custom_call" | custom-call | tf_op jit(solution)/shard_map/pack/pallas_call | solution.py:317
  1.8 11.5 %collective-permute-start.2 = (bf16[1040,128]{1,0:T(8,128)(2,1)}, bf16[1040,128]{1,0:T(8,128)(2,1)S(1)}, u32[]{:S(2)}, u32[]{:S(2)}) collective-permute-start(bf16[1040,128]{1,0:T(8,128)(2,1)} %get-tuple-element.11.refs_0_), channel_id=1, source_target_pairs={{0,48},{8,56},{16,0},{24,8},{32,16},{40,24},{48,32},{56,40},{64,11... | collective-permute-start | bytes 798728 | tf_op jit(solution)/shard_map/ppermute | solution.py:334
  13.3 1.9 %collective-permute-start.1 = (bf16[1040,128]{1,0:T(8,128)(2,1)}, bf16[1040,128]{1,0:T(8,128)(2,1)S(1)}, u32[]{:S(2)}, u32[]{:S(2)}) collective-permute-start(bf16[1040,128]{1,0:T(8,128)(2,1)} %get-tuple-element.11.refs_0_), channel_id=1, source_target_pairs={{0,32},{8,40},{16,48},{24,56},{32,0},{40,8},{48,16},{56,24},{64,96... | collective-permute-start | bytes 798728 | tf_op jit(solution)/shard_map/ppermute | solution.py:334
  15.2 4.2 %collective-permute-start = (bf16[1040,128]{1,0:T(8,128)(2,1)}, bf16[1040,128]{1,0:T(8,128)(2,1)S(1)}, u32[]{:S(2)}, u32[]{:S(2)}) collective-permute-start(bf16[1040,128]{1,0:T(8,128)(2,1)} %get-tuple-element.11.refs_0_), channel_id=1, source_target_pairs={{0,16},{8,24},{16,32},{24,40},{32,48},{40,56},{48,0},{56,8},{64,80... | collective-permute-start | bytes 798728 | tf_op jit(solution)/shard_map/ppermute | solution.py:334
  19.5 0.0 copy-start.1
  19.5 8.0 %all-to-all-start = ((bf16[16,32,128]{2,1,0:T(8,128)(2,1)}), bf16[16,32,128]{2,1,0:T(8,128)(2,1)S(1)}, u32[]{:S(2)}, u32[]{:S(2)}) async-start(bf16[16,32,128]{2,1,0:T(8,128)(2,1)} %get-tuple-element.10), calls=%async_computation | async-start | bytes 262144 | tf_op jit(solution)/shard_map/all_to_all | solution.py:251
  27.5 0.0 copy-start.4
  27.5 0.0 copy-start.5
  27.5 0.0 copy-start.6
  27.5 0.0 copy-start.2
  27.5 0.0 copy-start.3
  28.3 0.0 copy-done.4
  28.3 0.0 copy-done.5
  28.3 0.0 copy-done.6
  28.3 0.1 copy-done.2
  28.4 0.0 copy-done.3
  28.4 0.4 own.1
  28.8 7.2 %all-to-all-done.q_ref = bf16[16,32,128]{2,1,0:T(8,128)(2,1)S(1)} async-done(((bf16[16,32,128]{2,1,0:T(8,128)(2,1)}), bf16[16,32,128]{2,1,0:T(8,128)(2,1)S(1)}, u32[]{:S(2)}, u32[]{:S(2)}) %all-to-all-start) | async-done | bytes 131104 | tf_op jit(solution)/shard_map/all_to_all | solution.py:251
  35.9 0.0 collective-permute-done.2.refs_3_
  35.9 0.0 collective-permute-done.1.refs_2_
  35.9 0.0 collective-permute-done.refs_1_
  36.0 0.0 copy-done.1
  36.0 2.0 %prompt.1 = bf16[16,40,128]{2,1,0:T(8,128)(2,1)S(1)} custom-call(s32[1]{0:T(128)} %bitcast.place_ref, f32[32,128]{1,0:T(8,128)S(1)} %get-tuple-element.9.own_ref, bf16[16,32,128]{2,1,0:T(8,128)(2,1)S(1)} %all-to-all-done.q_ref, bf16[1040,128]{1,0:T(8,128)(2,1)S(1)} %copy-done.1, bf16[1040,128]{1,0:T(8,128)(2,1)S(1)} %collective-permute-done.refs_1_, ...), custom_call_target="tpu_custom_call" | custom-call | tf_op jit(solution)/shard_map/prompt/pallas_call | solution.py:345
  38.0 0.0 copy-start
  38.0 13.0 %all_to_all.20.part_ref = bf16[16,40,128]{2,1,0:T(8,128)(2,1)S(1)} all-to-all(bf16[16,40,128]{2,1,0:T(8,128)(2,1)S(1)} %prompt.1), channel_id=1, replica_groups={{0,8,64,72,128,136,192,200,256,264,320,328,384,392,448,456},{16,24,80,8..., dimensions={0} | all-to-all | bytes 327680 | tf_op jit(solution)/shard_map/all_to_all | solution.py:251
  51.0 0.2 combine.1
  51.2 23.2 %all_to_all.21.x_ref = bf16[64,32,128]{2,1,0:T(8,128)(2,1)S(1)} all-to-all(bf16[64,32,128]{2,1,0:T(8,128)(2,1)S(1)} %combine.1), channel_id=1, replica_groups={{0,88,176,264,352,440,16,104,192,280,368,456,32,120,208,296,384,472,48,..., dimensions={0} | all-to-all | bytes 1048576 | tf_op jit(solution)/shard_map/all_to_all | solution.py:251
  74.4 0.0 copy-done
  74.4 0.8 project.1
  75.2 13.0 %all_to_all.22.x_ref = f32[8,16,256]{2,1,0:T(8,128)S(1)} all-to-all(f32[8,16,256]{2,1,0:T(8,128)S(1)} %project.1), channel_id=1, replica_groups=mesh['ctx'=64,'head'=8] {'head'}, dimensions={0} | all-to-all | bytes 262144 | tf_op jit(solution)/shard_map/all_to_all | solution.py:251
  88.2 0.6 sum.1
Async XLA Ops:
  1.8 34.1 %collective-permute-start.2 = (bf16[1040,128]{1,0:T(8,128)(2,1)}, bf16[1040,128]{1,0:T(8,128)(2,1)S(1)}, u32[]{:S(2)}, u32[]{:S(2)}) collective-permute-start(bf16[1040,128]{1,0:T(8,128)(2,1)} %get-tuple-element.11.refs_0_), channel_id=1, source_target_pairs={{0,48},{8,56},{16,0},{24,8},{32,16},{40,24},{48,32},{56,40},{64,11... | collective-permute-start | bytes 798728 | tf_op jit(solution)/shard_map/ppermute | solution.py:334
  13.3 22.6 %collective-permute-start.1 = (bf16[1040,128]{1,0:T(8,128)(2,1)}, bf16[1040,128]{1,0:T(8,128)(2,1)S(1)}, u32[]{:S(2)}, u32[]{:S(2)}) collective-permute-start(bf16[1040,128]{1,0:T(8,128)(2,1)} %get-tuple-element.11.refs_0_), channel_id=1, source_target_pairs={{0,32},{8,40},{16,48},{24,56},{32,0},{40,8},{48,16},{56,24},{64,96... | collective-permute-start | bytes 798728 | tf_op jit(solution)/shard_map/ppermute | solution.py:334
  15.2 20.7 %collective-permute-start = (bf16[1040,128]{1,0:T(8,128)(2,1)}, bf16[1040,128]{1,0:T(8,128)(2,1)S(1)}, u32[]{:S(2)}, u32[]{:S(2)}) collective-permute-start(bf16[1040,128]{1,0:T(8,128)(2,1)} %get-tuple-element.11.refs_0_), channel_id=1, source_target_pairs={{0,16},{8,24},{16,32},{24,40},{32,48},{40,56},{48,0},{56,8},{64,80... | collective-permute-start | bytes 798728 | tf_op jit(solution)/shard_map/ppermute | solution.py:334
  19.5 16.5 %copy-start.1 = (bf16[1040,128]{1,0:T(8,128)(2,1)S(1)}, bf16[1040,128]{1,0:T(8,128)(2,1)}, u32[]{:S(2)}) copy-start(bf16[1040,128]{1,0:T(8,128)(2,1)} %get-tuple-element.11.refs_0_) | copy-start | bytes 798724
  19.5 16.5 %all-to-all-start = ((bf16[16,32,128]{2,1,0:T(8,128)(2,1)}), bf16[16,32,128]{2,1,0:T(8,128)(2,1)S(1)}, u32[]{:S(2)}, u32[]{:S(2)}) async-start(bf16[16,32,128]{2,1,0:T(8,128)(2,1)} %get-tuple-element.10), calls=%async_computation | async-start | bytes 262144 | tf_op jit(solution)/shard_map/all_to_all | solution.py:251
  27.5 0.8 copy-start.4
  27.5 0.8 copy-start.5
  27.5 0.8 copy-start.6
  27.5 0.9 copy-start.2
  27.5 0.9 copy-start.3
  38.0 36.4 %copy-start = (bf16[2048,256]{1,0:T(8,128)(2,1)S(1)}, bf16[2048,256]{1,0:T(8,128)(2,1)}, u32[]{:S(2)}) copy-start(bf16[2048,256]{1,0:T(8,128)(2,1)} %w_ref.1) | copy-start | bytes 3145732

commit v9 on v8

--- a/solution.py
+++ b/solution.py
@@ -358,7 +358,7 @@
     product = call(
         project_kernel,
         "project",
-        struct((heads, STEPS * samples // heads, columns), F32),
+        struct((heads, STEPS * samples // heads, columns), BF16),
         [VMEM] * 2,
         VMEM,
         [pltpu.VMEM((samples * ITEM, HD), F32)],

time: 89.6 us -> 89.1 us (level)
  no operation moved by 1% of the time
where the time goes in v9:
time: 89.1 us; the launch traced here: 88.4 us
  blocking collectives  48.8 us (55%)
  starting transfers between devices  25.6 us (29%)
  waiting for transfers between devices  7.19 us (8%)
  Pallas kernels  5.82 us (7%)
    all_to_all x3, blocking collectives, swap(): lax.all_to_all(array, axes, split_axis=0, concat_axis=0, axis_index_group...  48.8 us
    ppermute x3, starting transfers between devices, shards(): packs.append(lax.ppermute(here, BOTH, hops(count)))  17.6 us
    all_to_all x1, starting transfers between devices, swap(): lax.all_to_all(array, axes, split_axis=0, concat_axis=0, axis_index_group...  7.98 us
    all_to_all x1, waiting for transfers between devices, swap(): lax.all_to_all(array, axes, split_axis=0, concat_axis=0, axis_index_group...  7.18 us
    pallas_call x1, Pallas kernels, shards(): call(prompt_kernel, 'prompt', struct((far, ITEM + STAT, HD), BF16), [SMEM...  2.02 us
    pallas_call x1, Pallas kernels, shards(): call(pack_kernel, 'pack', (struct((far, ITEM, HD), BF16), struct((2 * tok...  1.8 us
  transfers between devices with their start and end apart: 4, of which 1 were waited for; matrix products, arithmetic and copies ran while one was open for 0% of the time, Pallas kernels for 0%

profile of v9, /device:TPU:1, one launch (start us, length us, event | category | flops | bytes accessed | tf_op | source)
XLA Modules:
  0.0 88.4 jit_solution(14278239686533268184)
XLA Ops:
  0.0 1.8 %pack.1 = (bf16[16,32,128]{2,1,0:T(8,128)(2,1)}, bf16[1040,128]{1,0:T(8,128)(2,1)}) custom-call(bf16[2,2048]{1,0:T(2,128)(2,1)} %bitcast.11, bf16[512,128]{1,0:T(8,128)(2,1)} %k_hbm.1, bf16[512,128]{1,0:T(8,128)(2,1)} %v_hbm.1, s32[8,64]{1,0:T(8,128)} %bitcast.15), custom_call_target="tpu_custom_call" | custom-call | tf_op jit(solution)/shard_map/pack/pallas_call | solution.py:317
  1.8 11.5 %collective-permute-start.2 = (bf16[1040,128]{1,0:T(8,128)(2,1)}, bf16[1040,128]{1,0:T(8,128)(2,1)S(1)}, u32[]{:S(2)}, u32[]{:S(2)}) collective-permute-start(bf16[1040,128]{1,0:T(8,128)(2,1)} %get-tuple-element.11.refs_0_), channel_id=1, source_target_pairs={{0,48},{8,56},{16,0},{24,8},{32,16},{40,24},{48,32},{56,40},{64,11... | collective-permute-start | bytes 798728 | tf_op jit(solution)/shard_map/ppermute | solution.py:334
  13.3 1.9 %collective-permute-start.1 = (bf16[1040,128]{1,0:T(8,128)(2,1)}, bf16[1040,128]{1,0:T(8,128)(2,1)S(1)}, u32[]{:S(2)}, u32[]{:S(2)}) collective-permute-start(bf16[1040,128]{1,0:T(8,128)(2,1)} %get-tuple-element.11.refs_0_), channel_id=1, source_target_pairs={{0,32},{8,40},{16,48},{24,56},{32,0},{40,8},{48,16},{56,24},{64,96... | collective-permute-start | bytes 798728 | tf_op jit(solution)/shard_map/ppermute | solution.py:334
  15.2 4.2 %collective-permute-start = (bf16[1040,128]{1,0:T(8,128)(2,1)}, bf16[1040,128]{1,0:T(8,128)(2,1)S(1)}, u32[]{:S(2)}, u32[]{:S(2)}) collective-permute-start(bf16[1040,128]{1,0:T(8,128)(2,1)} %get-tuple-element.11.refs_0_), channel_id=1, source_target_pairs={{0,16},{8,24},{16,32},{24,40},{32,48},{40,56},{48,0},{56,8},{64,80... | collective-permute-start | bytes 798728 | tf_op jit(solution)/shard_map/ppermute | solution.py:334
  19.5 0.0 copy-start.1
  19.5 8.0 %all-to-all-start = ((bf16[16,32,128]{2,1,0:T(8,128)(2,1)}), bf16[16,32,128]{2,1,0:T(8,128)(2,1)S(1)}, u32[]{:S(2)}, u32[]{:S(2)}) async-start(bf16[16,32,128]{2,1,0:T(8,128)(2,1)} %get-tuple-element.10), calls=%async_computation | async-start | bytes 262144 | tf_op jit(solution)/shard_map/all_to_all | solution.py:251
  27.5 0.0 copy-start.4
  27.5 0.0 copy-start.5
  27.5 0.0 copy-start.6
  27.5 0.0 copy-start.2
  27.5 0.0 copy-start.3
  28.3 0.0 copy-done.4
  28.3 0.0 copy-done.5
  28.3 0.0 copy-done.6
  28.3 0.1 copy-done.2
  28.4 0.0 copy-done.3
  28.4 0.4 own.1
  28.8 7.2 %all-to-all-done.q_ref = bf16[16,32,128]{2,1,0:T(8,128)(2,1)S(1)} async-done(((bf16[16,32,128]{2,1,0:T(8,128)(2,1)}), bf16[16,32,128]{2,1,0:T(8,128)(2,1)S(1)}, u32[]{:S(2)}, u32[]{:S(2)}) %all-to-all-start) | async-done | bytes 131104 | tf_op jit(solution)/shard_map/all_to_all | solution.py:251
  35.9 0.0 collective-permute-done.2.refs_3_
  35.9 0.0 collective-permute-done.1.refs_2_
  35.9 0.0 collective-permute-done.refs_1_
  36.0 0.0 copy-done.1
  36.0 2.0 %prompt.1 = bf16[16,40,128]{2,1,0:T(8,128)(2,1)S(1)} custom-call(s32[1]{0:T(128)} %bitcast.place_ref, f32[32,128]{1,0:T(8,128)S(1)} %get-tuple-element.9.own_ref, bf16[16,32,128]{2,1,0:T(8,128)(2,1)S(1)} %all-to-all-done.q_ref, bf16[1040,128]{1,0:T(8,128)(2,1)S(1)} %copy-done.1, bf16[1040,128]{1,0:T(8,128)(2,1)S(1)} %collective-permute-done.refs_1_, ...), custom_call_target="tpu_custom_call" | custom-call | tf_op jit(solution)/shard_map/prompt/pallas_call | solution.py:345
  38.0 0.0 copy-start
  38.0 13.0 %all_to_all.20.part_ref = bf16[16,40,128]{2,1,0:T(8,128)(2,1)S(1)} all-to-all(bf16[16,40,128]{2,1,0:T(8,128)(2,1)S(1)} %prompt.1), channel_id=1, replica_groups={{0,8,64,72,128,136,192,200,256,264,320,328,384,392,448,456},{16,24,80,8..., dimensions={0} | all-to-all | bytes 327680 | tf_op jit(solution)/shard_map/all_to_all | solution.py:251
  51.0 0.2 combine.1
  51.2 23.2 %all_to_all.21.x_ref = bf16[64,32,128]{2,1,0:T(8,128)(2,1)S(1)} all-to-all(bf16[64,32,128]{2,1,0:T(8,128)(2,1)S(1)} %combine.1), channel_id=1, replica_groups={{0,88,176,264,352,440,16,104,192,280,368,456,32,120,208,296,384,472,48,..., dimensions={0} | all-to-all | bytes 1048576 | tf_op jit(solution)/shard_map/all_to_all | solution.py:251
  74.4 0.0 copy-done
  74.4 0.8 project.1
  75.2 12.6 %all_to_all.22.x_ref = bf16[8,16,256]{2,1,0:T(8,128)(2,1)S(1)} all-to-all(bf16[8,16,256]{2,1,0:T(8,128)(2,1)S(1)} %project.1), channel_id=1, replica_groups=mesh['ctx'=64,'head'=8] {'head'}, dimensions={0} | all-to-all | bytes 131072 | tf_op jit(solution)/shard_map/all_to_all | solution.py:251
  87.8 0.6 sum.1
Async XLA Ops:
  1.8 34.1 %collective-permute-start.2 = (bf16[1040,128]{1,0:T(8,128)(2,1)}, bf16[1040,128]{1,0:T(8,128)(2,1)S(1)}, u32[]{:S(2)}, u32[]{:S(2)}) collective-permute-start(bf16[1040,128]{1,0:T(8,128)(2,1)} %get-tuple-element.11.refs_0_), channel_id=1, source_target_pairs={{0,48},{8,56},{16,0},{24,8},{32,16},{40,24},{48,32},{56,40},{64,11... | collective-permute-start | bytes 798728 | tf_op jit(solution)/shard_map/ppermute | solution.py:334
  13.3 22.6 %collective-permute-start.1 = (bf16[1040,128]{1,0:T(8,128)(2,1)}, bf16[1040,128]{1,0:T(8,128)(2,1)S(1)}, u32[]{:S(2)}, u32[]{:S(2)}) collective-permute-start(bf16[1040,128]{1,0:T(8,128)(2,1)} %get-tuple-element.11.refs_0_), channel_id=1, source_target_pairs={{0,32},{8,40},{16,48},{24,56},{32,0},{40,8},{48,16},{56,24},{64,96... | collective-permute-start | bytes 798728 | tf_op jit(solution)/shard_map/ppermute | solution.py:334
  15.2 20.7 %collective-permute-start = (bf16[1040,128]{1,0:T(8,128)(2,1)}, bf16[1040,128]{1,0:T(8,128)(2,1)S(1)}, u32[]{:S(2)}, u32[]{:S(2)}) collective-permute-start(bf16[1040,128]{1,0:T(8,128)(2,1)} %get-tuple-element.11.refs_0_), channel_id=1, source_target_pairs={{0,16},{8,24},{16,32},{24,40},{32,48},{40,56},{48,0},{56,8},{64,80... | collective-permute-start | bytes 798728 | tf_op jit(solution)/shard_map/ppermute | solution.py:334
  19.5 16.5 %copy-start.1 = (bf16[1040,128]{1,0:T(8,128)(2,1)S(1)}, bf16[1040,128]{1,0:T(8,128)(2,1)}, u32[]{:S(2)}) copy-start(bf16[1040,128]{1,0:T(8,128)(2,1)} %get-tuple-element.11.refs_0_) | copy-start | bytes 798724
  19.5 16.5 %all-to-all-start = ((bf16[16,32,128]{2,1,0:T(8,128)(2,1)}), bf16[16,32,128]{2,1,0:T(8,128)(2,1)S(1)}, u32[]{:S(2)}, u32[]{:S(2)}) async-start(bf16[16,32,128]{2,1,0:T(8,128)(2,1)} %get-tuple-element.10), calls=%async_computation | async-start | bytes 262144 | tf_op jit(solution)/shard_map/all_to_all | solution.py:251
  27.5 0.8 copy-start.4
  27.5 0.8 copy-start.5
  27.5 0.8 copy-start.6
  27.5 0.9 copy-start.2
  27.5 0.9 copy-start.3
  38.0 36.4 %copy-start = (bf16[2048,256]{1,0:T(8,128)(2,1)S(1)}, bf16[2048,256]{1,0:T(8,128)(2,1)}, u32[]{:S(2)}) copy-start(bf16[2048,256]{1,0:T(8,128)(2,1)} %w_ref.1) | copy-start | bytes 3145732
